TPU v7x, 512 devices: a whole 4x4x16 slice. The times are simulated.
512 devices in a mesh: half: 2 (over core), grp: 256 (over x, y, z).
Axes of the slice: x: 4, y: 4, z: 16, core: 2. Of those that a mesh axis runs over, the one named last changes fastest.
Arguments:
- images: bfloat16 [131072, 2048], P(('half', 'grp')), parts along dimension 0, may hold values from -6 to 6
- projection: bfloat16 [4096, 256], replicated, may hold values from -0.375 to 0.375
- volume: bfloat16 [512, 2048], P(('half', 'grp')), parts along dimension 0, may hold values from -6 to 6
- subset: int32 [512, 1024], P(('half', 'grp')), parts along dimension 0, may hold values from 0 to 4095, all different within a row
- precision: float32 [131072], P(('half', 'grp')), parts along dimension 0, may hold values from 0.005 to 0.3
Outputs:
- new_volume: float32 [512, 2048], P(('half', 'grp')), parts along dimension 0
- log_evidence: float32 [131072], P(('half', 'grp')), parts along dimension 0
There are 2 independent parts, one for each index of `half`. A program takes and returns all parts, laid end to end along the dimension named above; an argument that names none is the same for every part. Nothing has to cross between parts.
Inputs may be any that keep to these rules, and one draw needn't show every extreme that they name: `subset`: each row holds 1024 different orientations, and every orientation is searched by some block.
All inputs are finite; a program needn't handle non-finite values.
Results may differ from a plain program's by a relative error of at most 0.025.
Values may be sent and summed in bfloat16 or wider, within the bound.
No kernel may reach another device: no remote copies, remote signals or barrier semaphores. Data moves between devices by JAX's collectives and lax.ppermute only.
A program may use at most 64 MiB of HBM per device.

v0:
```python
import jax
import jax.numpy as jnp
from jax import lax
from jax.sharding import PartitionSpec as P


def local(images, projection, volume, subset, precision):
    picked = jnp.take(projection, subset[0], axis=0)
    gathered = lax.all_gather(volume, "grp", axis=0, tiled=True)
    templ_full = jnp.dot(picked, gathered, preferred_element_type=jnp.float32)
    templates = templ_full.astype(jnp.bfloat16)
    tfloat = templates.astype(jnp.float32)
    energy = jnp.sum(tfloat * tfloat, axis=1)
    correlate = lax.dot_general(
        images, templates, (((1,), (1,)), ((), ())), preferred_element_type=jnp.float32
    )
    scores = precision[:, None] * (correlate - 0.5 * energy[None, :])
    highest = jnp.max(scores, axis=1, keepdims=True)
    summed = jnp.sum(jnp.exp(scores - highest), axis=1, keepdims=True)
    evidence = highest + jnp.log(summed)
    weights = jnp.exp(scores - evidence)
    weights_low = weights.astype(jnp.bfloat16)
    backproj = lax.dot_general(
        weights_low, images, (((0,), (0,)), ((), ())), preferred_element_type=jnp.float32
    ).astype(jnp.bfloat16)
    occupancy = jnp.sum(weights, axis=0)
    numerator = lax.dot_general(
        picked, backproj, (((0,), (0,)), ((), ())), preferred_element_type=jnp.float32
    )
    pfloat = picked.astype(jnp.float32)
    slab_weight = jnp.dot(occupancy, pfloat * pfloat, precision=lax.Precision.HIGHEST)
    numer_mine, weight_mine = (
        lax.psum_scatter(numerator, "grp", scatter_dimension=0, tiled=True),
        lax.psum_scatter(slab_weight, "grp", scatter_dimension=0, tiled=True),
    )
    new_volume = numer_mine / (weight_mine[:, None] + 1.0)
    return (new_volume, evidence[:, 0])


def solution(mesh):
    placed = (
        P(("half", "grp"), None),
        P(),
        P(("half", "grp"), None),
        P(("half", "grp"), None),
        P(("half", "grp")),
    )
    return jax.shard_map(
        local,
        mesh=mesh,
        in_specs=placed,
        out_specs=(P(("half", "grp"), None), P(("half", "grp"))),
        check_vma=False,
    )
```

profile of v0, /device:TPU:0, one launch (start us, length us, event | category | flops | bytes accessed | tf_op | source)
XLA Modules:
  0.0 921.4 jit_solution(5265334927013490296)
XLA Ops:
  7.2 0.0 copy-start
  7.2 0.0 copy-start.2
  7.2 0.0 all-gather.3.cloned.1.call-start
  7.2 0.7 all-gather.3.cloned.1.call-update
  7.9 0.0 all-reduce.4.cloned.1.call-start
  8.0 0.7 compare_select_fusion
  8.7 0.1 copy-done
  8.8 3.9 gather_fusion
  12.7 0.0 copy-start.1
  12.7 0.0 copy-done.2
  12.7 0.0 copy-start.5
  12.7 194.7 %all-gather.3.cloned.1.call-done = bf16[256,1,2048]{2,1,0:T(2,128)(2,1)} async-done(((bf16[1,1,2048]{2,1,0:T(2,128)(2,1)}), bf16[256,1,2048]{2,1,0:T(2,128)(2,1)}) %all-gather.3.cloned.1.call-update) | async-done | bytes 1048592 | tf_op jit(solution)/shard_map/all_gather | solution.py:9
  207.4 0.0 copy-start.4
  207.4 4.1 multiply_reduce_fusion
  211.6 0.0 copy-done.1
  211.6 0.0 copy-done.5
  211.6 0.0 copy-done.4
  211.6 1.3 fusion.16
  212.9 0.2 exponential_reduce_fusion
  213.2 0.0 copy-start.3
  213.2 5.0 fusion
  218.2 0.0 all-reduce.4.cloned.1.call-update
  218.2 1.2 dynamic-slice
  219.5 0.0 copy-done.3
  219.5 0.2 fusion.10
  219.7 1.7 fusion.7
  221.4 689.3 %all-reduce.1 = f32[256]{0:T(256)S(1)} all-reduce(f32[256]{0:T(256)S(1)} %bitcast.22), channel_id=3, replica_groups=mesh['half'=2,'grp'=256] {'grp'}, use_global_device_ids=true, to_apply=%region_5.6.clone | all-reduce | flops 256 | bytes 2048
  910.7 1.1 dynamic-slice.3
  912.5 0.0 all-reduce.4.cloned.1.call-done
  912.5 2.0 dynamic-slice_divide_fusion
  (4 shorter events, 0.0 us)
Async XLA Ops:
  7.2 1.6 copy-start
  7.2 5.5 copy-start.2
  7.2 200.2 %all-gather.3.cloned.1.call-start = ((), (), s32[]{:S(2)}) async-start(), calls=%async_computation | async-start | bytes 2105344 | tf_op jit(solution)/shard_map/all_gather | solution.py:9
  7.9 904.6 %all-reduce.4.cloned.1.call-start = ((), (), s32[]{:S(2)}) async-start(), calls=%async_computation.1 | async-start | bytes 4194304
  12.7 198.9 %copy-start.1 = (bf16[1024,256]{1,0:T(8,128)(2,1)}, bf16[1024,256]{1,0:T(8,128)(2,1)S(1)}, u32[]{:S(2)}) copy-start(bf16[1024,256]{1,0:T(8,128)(2,1)S(1)} %gather_fusion) | copy-start | bytes 1572868
  12.7 198.8 %copy-start.5 = (f32[256]{0:T(256)S(1)}, f32[256]{0:T(256)}, u32[]{:S(2)}) copy-start(f32[256]{0:T(256)} %param.9) | copy-start | bytes 3076
  207.4 4.2 copy-start.4
  213.2 6.3 copy-start.3
Sparse Core Ops, SparseCore 0:
  12.3 195.0 all-gather.2
  218.3 405.5 all-reduce.3
where the time goes:
time: 922 us; the launch traced here: 921 us
  blocking collectives  689 us (75%)
  waiting for transfers between devices  195 us (21%)
  between operations  14.8 us (2%)
  matrix products  12.2 us (1%)
    unnamed x1, blocking collectives  689 us
    all_gather x1, waiting for transfers between devices, local(): gathered = lax.all_gather(volume, 'grp', axis=0, tiled=True)  195 us
  transfers between devices with their start and end apart: 2, of which 1 were waited for; matrix products, arithmetic and copies ran while one was open for 1% of the time, Pallas kernels for 0%

commit v1 on v0

--- a/solution.py
+++ b/solution.py
@@ -1,12 +1,34 @@
 import jax
 import jax.numpy as jnp
 from jax import lax
-from jax.sharding import PartitionSpec as P
+from jax.sharding import Mesh, PartitionSpec as P
+
+X, Y, Z = 4, 4, 16
+PLANE = ("x", "y")
+
+
+def gather_slabs(volume):
+    column = lax.all_to_all(
+        jnp.broadcast_to(volume.reshape(1, 16, 128), (Z, 16, 128)), "z", 0, 0, tiled=True
+    )
+    column = column.reshape(Z, 2048)
+    whole = lax.all_to_all(
+        jnp.broadcast_to(column[None], (X * Y, Z, 2048)), PLANE, 0, 0, tiled=True
+    )
+    return whole.reshape(X * Y * Z, 2048)
+
+
+def sum_slabs(partial):
+    width = partial.shape[1]
+    plane = lax.all_to_all(partial.reshape(X * Y, Z, width), PLANE, 0, 0, tiled=True)
+    plane = jnp.sum(plane.astype(jnp.float32), axis=0).astype(jnp.bfloat16)
+    column = lax.all_to_all(plane.reshape(Z, width // 128, 128), "z", 0, 0, tiled=True)
+    return jnp.sum(column.astype(jnp.float32), axis=0).reshape(1, width)
 
 
 def local(images, projection, volume, subset, precision):
     picked = jnp.take(projection, subset[0], axis=0)
-    gathered = lax.all_gather(volume, "grp", axis=0, tiled=True)
+    gathered = gather_slabs(volume)
     templ_full = jnp.dot(picked, gathered, preferred_element_type=jnp.float32)
     templates = templ_full.astype(jnp.bfloat16)
     tfloat = templates.astype(jnp.float32)
@@ -29,26 +51,25 @@
     )
     pfloat = picked.astype(jnp.float32)
     slab_weight = jnp.dot(occupancy, pfloat * pfloat, precision=lax.Precision.HIGHEST)
-    numer_mine, weight_mine = (
-        lax.psum_scatter(numerator, "grp", scatter_dimension=0, tiled=True),
-        lax.psum_scatter(slab_weight, "grp", scatter_dimension=0, tiled=True),
+    high = slab_weight.astype(jnp.bfloat16)
+    rest = (slab_weight - high.astype(jnp.float32)).astype(jnp.bfloat16)
+    extra = jnp.concatenate(
+        [high[:, None], rest[:, None], jnp.zeros((256, 126), jnp.bfloat16)], axis=1
     )
-    new_volume = numer_mine / (weight_mine[:, None] + 1.0)
+    mine = sum_slabs(jnp.concatenate([numerator.astype(jnp.bfloat16), extra], axis=1))
+    weight_mine = mine[:, 2048:2049] + mine[:, 2049:2050]
+    new_volume = mine[:, :2048] / (weight_mine + 1.0)
     return (new_volume, evidence[:, 0])
 
 
 def solution(mesh):
-    placed = (
-        P(("half", "grp"), None),
-        P(),
-        P(("half", "grp"), None),
-        P(("half", "grp"), None),
-        P(("half", "grp")),
-    )
+    grid = Mesh(mesh.devices.reshape(2, X, Y, Z), ("half", "x", "y", "z"))
+    every = ("half", "x", "y", "z")
+    placed = (P(every, None), P(), P(every, None), P(every, None), P(every))
     return jax.shard_map(
         local,
-        mesh=mesh,
+        mesh=grid,
         in_specs=placed,
-        out_specs=(P(("half", "grp"), None), P(("half", "grp"))),
+        out_specs=(P(every, None), P(every)),
         check_vma=False,
     )

time: 922 us -> 107 us (0.12)
  the two profiles are of different devices: /device:TPU:0 before, /device:TPU:32 now
where the time goes in v1:
time: 107 us; the launch traced here: 106 us
  blocking collectives  62.6 us (59%)
  waiting for transfers between devices  10.7 us (10%)
  matrix products  10.3 us (10%)
  local copies, waits for them, and re-layouts  9.58 us (9%)
  starting transfers between devices  7.03 us (7%)
  other arithmetic  4.08 us (4%)
  between operations  2.11 us (2%)
    all_to_all x1, blocking collectives, gather_slabs(): lax.all_to_all(jnp.broadcast_to(volume.reshape(1, 16, 128), (Z, 16, 128))...  26.5 us
    all_to_all x1, blocking collectives, sum_slabs(): lax.all_to_all(partial.reshape(X * Y, Z, width), PLANE, 0, 0, tiled=True)  19.7 us
    all_to_all x1, blocking collectives, sum_slabs(): lax.all_to_all(plane.reshape(Z, width // 128, 128), 'z', 0, 0, tiled=True)  16.4 us
    all_to_all x1, waiting for transfers between devices, gather_slabs(): lax.all_to_all(jnp.broadcast_to(column[None], (X * Y, Z, 2048)), PLANE, 0...  10.7 us
    all_to_all x1, starting transfers between devices, gather_slabs(): lax.all_to_all(jnp.broadcast_to(column[None], (X * Y, Z, 2048)), PLANE, 0...  7.03 us
    gather x1, local copies, waits for them, and re-layouts, local(): picked = jnp.take(projection, subset[0], axis=0)  4.94 us
    dot_general x1, matrix products, local(): lax.dot_general(picked, backproj, (((0,), (0,)), ((), ())), preferred_ele...  4.73 us
    concatenate x3, local copies, waits for them, and re-layouts, local(): jnp.concatenate([numerator.astype(jnp.bfloat16), extra], axis=1)  2.81 us
  transfers between devices with their start and end apart: 1, of which 1 were waited for; matrix products, arithmetic and copies ran while one was open for 5% of the time, Pallas kernels for 0%

profile of v1, /device:TPU:32, one launch (start us, length us, event | category | flops | bytes accessed | tf_op | source)
XLA Modules:
  0.0 106.4 jit_solution(11741234704260375898)
XLA Ops:
  0.6 0.0 copy-start
  0.6 0.0 copy-start.1
  0.7 0.9 reduce.4
  1.5 26.5 %all_to_all.20 = bf16[16,16,128]{2,1,0:T(8,128)(2,1)S(1)} all-to-all(bf16[16,16,128]{2,1,0:T(8,128)(2,1)S(1)} %broadcast_in_dim.36), channel_id=1, replica_groups=mesh['half'=2,'x'=4,'y'=4,'z'=16] {'z'}, dimensions={0} | all-to-all | bytes 131072 | tf_op jit(solution)/shard_map/all_to_all | solution.py:11
  28.1 1.1 %broadcast_in_dim.38 = bf16[16,16,2048]{2,1,0:T(8,128)(2,1)} broadcast(bf16[16,2048]{1,0:T(8,128)(2,1)S(1)} %bitcast.26), dimensions={1,2} | broadcast | bytes 1114112 | tf_op jit(solution)/shard_map/broadcast_in_dim | solution.py:16
  29.2 7.0 %all-to-all-start.1 = ((bf16[16,16,2048]{2,1,0:T(8,128)(2,1)}), bf16[16,16,2048]{2,1,0:T(8,128)(2,1)S(1)}, u32[]{:S(2)}, u32[]{:S(2)}) async-start(bf16[16,16,2048]{2,1,0:T(8,128)(2,1)} %broadcast_in_dim.38), calls=%async_computation.1 | async-start | bytes 2097152 | tf_op jit(solution)/shard_map/all_to_all | solution.py:15
  36.3 0.7 compare_select_fusion
  37.0 0.0 copy-done
  37.0 4.9 %gather_fusion = bf16[1024,256]{1,0:T(8,128)(2,1)} fusion(bf16[4096,256]{1,0:T(8,128)(2,1)S(1)} %copy-done, s32[1024]{0:T(1024)S(1)} %broadcast_clamp_fusion), kind=kCustom, calls=%fused_computation | custom fusion | bytes 1052672 | tf_op jit(solution)/shard_map/jit(_take)/gather | solution.py:30
  41.9 0.0 copy-done.1
  41.9 10.7 %all-to-all-done.1 = bf16[16,16,2048]{2,1,0:T(8,128)(2,1)S(1)} async-done(((bf16[16,16,2048]{2,1,0:T(8,128)(2,1)}), bf16[16,16,2048]{2,1,0:T(8,128)(2,1)S(1)}, u32[]{:S(2)}, u32[]{:S(2)}) %all-to-all-start.1) | async-done | bytes 1048608 | tf_op jit(solution)/shard_map/all_to_all | solution.py:15
  52.6 0.0 copy-start.3
  52.6 0.0 copy-start.4
  52.6 2.5 %multiply_reduce_fusion = (f32[1024]{0:T(1024)S(1)}, bf16[1024,2048]{1,0:T(8,128)(2,1)S(1)}) fusion(bf16[256,2048]{1,0:T(8,128)(2,1)S(1)} %bitcast.24, bf16[1024,256]{1,0:T(8,128)(2,1)} %gather_fusion, pred[1024]{0:T(1024)(128)(4,1)S(1)} %compare_and_fusion), kind=kOutput, calls=%fused_computation.1 | convolution fusion | flops 1082391552 | bytes 5772288 | tf_op jit(solution)/shard_map/dot_general | solution.py:32
  55.1 0.0 copy-done.3
  55.1 0.0 copy-done.4
  55.1 1.3 %fusion.18 = (f32[256]{0:T(256)S(1)}, f32[1024,256]{1,0:T(8,128)S(1)}) fusion(f32[1024]{0:T(1024)S(1)} %broadcast_multiply_fusion, bf16[1024,2048]{1,0:T(8,128)(2,1)S(1)} %get-tuple-element.7, bf16[256,2048]{1,0:T(8,128)(2,1)S(1)} %copy-done.3, f32[256]{0:T(256)S(1)} %copy-done.4), kind=kOutput, calls=%fused_computation.30 | convolution fusion | flops 1074528000 | bytes 6297600 | tf_op jit(solution)/shard_map/dot_general | solution.py:36
  56.5 0.2 exponential_reduce_fusion
  56.7 0.0 copy-start.2
  56.7 0.2 fusion.11
  57.0 4.7 %fusion.4 = bf16[256,2048]{1,0:T(8,128)(2,1)} fusion(bf16[256,2048]{1,0:T(8,128)(2,1)} %param.5, f32[1024,256]{1,0:T(8,128)S(1)} %get-tuple-element.9, f32[256]{0:T(256)S(1)} %log_add_fusion, bf16[1024,256]{1,0:T(8,128)(2,1)} %gather_fusion, pred[1024]{0:T(1024)(128)(4,1)S(1)} %compare_and_fusion), kind=kOutput, calls=%fused_computation.6 | convolution fusion | flops 2150891520 | bytes 3672064 | tf_op jit(solution)/shard_map/dot_general | solution.py:49
  61.7 0.0 copy-done.2
  61.7 1.7 %fusion.8 = f32[1,256]{1,0:T(1,128)S(1)} fusion(f32[1024,1]{0,1:T(1,128)S(1)} %bitcast.34, bf16[1024,256]{1,0:T(8,128)(2,1)} %gather_fusion, pred[1024]{0:T(1024)(128)(4,1)S(1)} %compare_and_fusion), kind=kOutput, calls=%fused_computation.9 | convolution fusion | flops 3932160 | bytes 530432 | tf_op jit(solution)/shard_map/dot_general | solution.py:53
  63.4 0.2 concatenate.14
  63.7 0.2 concatenate.15
  64.0 2.3 %concatenate.13 = bf16[16,16,2176]{2,1,0:T(8,128)(2,1)S(1)} concatenate(bf16[16,16,2048]{2,1,0:T(8,128)(2,1)} %bitcast.25, bf16[16,16,1]{2,1,0:T(8,128)(2,1)S(1)} %concatenate.14, bf16[16,16,1]{2,1,0:T(8,128)(2,1)S(1)} %concatenate.15, bf16[16,16,126]{2,1,0:T(8,128)(2,1)S(1)} %broadcast_in_dim.39), dimensions={2} | concatenate | bytes 2228224 | tf_op jit(solution)/shard_map/concatenate | solution.py:59
  66.3 19.7 %all_to_all.21 = bf16[16,16,2176]{2,1,0:T(8,128)(2,1)} all-to-all(bf16[16,16,2176]{2,1,0:T(8,128)(2,1)S(1)} %concatenate.13), channel_id=1, replica_groups=mesh['half'=2,'x'=4,'y'=4,'z'=16] {'x','y'}, dimensions={0} | all-to-all | bytes 2228224 | tf_op jit(solution)/shard_map/all_to_all | solution.py:23
  86.0 1.4 %reduce_sum.51 = bf16[16,2176]{1,0:T(8,128)(2,1)S(1)} reduce(bf16[16,16,2176]{2,1,0:T(8,128)(2,1)} %all_to_all.21, bf16[]{:T(256)} %constant.25.clone.1), dimensions={0}, to_apply=%region_4.5 | reduce | flops 522240 | bytes 1183746 | tf_op jit(solution)/shard_map/reduce_sum | solution.py:24
  87.5 16.4 %all_to_all.22 = bf16[16,17,128]{2,1,0:T(8,128)(2,1)S(1)} all-to-all(bf16[16,17,128]{2,1,0:T(8,128)(2,1)S(1)} %reshape.74), channel_id=1, replica_groups=mesh['half'=2,'x'=4,'y'=4,'z'=16] {'z'}, dimensions={0} | all-to-all | bytes 139264 | tf_op jit(solution)/shard_map/all_to_all | solution.py:25
  103.9 0.6 fusion.17
  105.8 0.6 slice_divide_fusion
  (11 shorter events, 0.2 us)
Async XLA Ops:
  0.6 36.3 %copy-start = (bf16[4096,256]{1,0:T(8,128)(2,1)S(1)}, bf16[4096,256]{1,0:T(8,128)(2,1)}, u32[]{:S(2)}) copy-start(bf16[4096,256]{1,0:T(8,128)(2,1)} %param.6) | copy-start | bytes 6291460
  0.6 41.3 %copy-start.1 = (s32[1,1024]{1,0:T(1,128)S(1)}, s32[1,1024]{1,0:T(1,128)}, u32[]{:S(2)}) copy-start(s32[1,1024]{1,0:T(1,128)} %param.8) | copy-start | bytes 12292
  29.2 23.4 %all-to-all-start.1 = ((bf16[16,16,2048]{2,1,0:T(8,128)(2,1)}), bf16[16,16,2048]{2,1,0:T(8,128)(2,1)S(1)}, u32[]{:S(2)}, u32[]{:S(2)}) async-start(bf16[16,16,2048]{2,1,0:T(8,128)(2,1)} %broadcast_in_dim.38), calls=%async_computation.1 | async-start | bytes 2097152 | tf_op jit(solution)/shard_map/all_to_all | solution.py:15
  52.6 2.5 %copy-start.3 = (bf16[256,2048]{1,0:T(8,128)(2,1)S(1)}, bf16[256,2048]{1,0:T(8,128)(2,1)}, u32[]{:S(2)}) copy-start(bf16[256,2048]{1,0:T(8,128)(2,1)} %param.5) | copy-start | bytes 3145732
  52.6 2.5 %copy-start.4 = (f32[256]{0:T(256)S(1)}, f32[256]{0:T(256)}, u32[]{:S(2)}) copy-start(f32[256]{0:T(256)} %param.9) | copy-start | bytes 3076
  56.7 5.0 %copy-start.2 = (f32[256]{0:T(256)}, f32[256]{0:T(256)S(1)}, u32[]{:S(2)}) copy-start(f32[256]{0:T(256)S(1)} %log_add_fusion) | copy-start | bytes 3076

commit v2 on v1

v2 whole, which is shorter than its diff:
```python
import jax
import jax.numpy as jnp
from jax import lax
from jax.experimental import pallas as pl
from jax.experimental.pallas import tpu as pltpu
from jax.sharding import Mesh, PartitionSpec as P

X, Y, Z = 4, 4, 16
PLANE = ("x", "y")
SLABS, FREQ, ORI, SUB, ROWS = 256, 2048, 4096, 1024, 256
WIDE = FREQ + 128
BF16, F32 = jnp.bfloat16, jnp.float32
NN = (((1,), (0,)), ((), ()))
NT = (((1,), (1,)), ((), ()))
TN = (((0,), (0,)), ((), ()))


def mm(a, b, dims):
    return lax.dot_general(a, b, dims, preferred_element_type=F32)


def parts(a, count):
    found = []
    for _ in range(count):
        found.append(a.astype(BF16))
        a = a - found[-1].astype(F32)
    return found


def pick_kernel(subset_ref, projection_ref, picked_ref, total_ref):
    subset = subset_ref[...]
    block = subset // 256
    within = subset - block * 256
    rows = lax.broadcasted_iota(jnp.int32, (256, SUB), 0).astype(F32).astype(BF16)
    for k in range(ORI // 256):
        wanted = jnp.where(block == k, within, -1).astype(F32).astype(BF16)
        chosen = jnp.where(rows == wanted, jnp.ones((), BF16), jnp.zeros((), BF16))
        part = mm(projection_ref[k * 256 : (k + 1) * 256, :], chosen, TN)
        if k == 0:
            total_ref[...] = part
        else:
            total_ref[...] += part
    picked_ref[...] = total_ref[...].astype(BF16)


def pick(subset, projection):
    return pl.pallas_call(
        pick_kernel,
        out_shape=jax.ShapeDtypeStruct((SLABS, SUB), BF16),
        in_specs=[pl.BlockSpec(memory_space=pltpu.VMEM)] * 2,
        out_specs=pl.BlockSpec(memory_space=pltpu.VMEM),
        scratch_shapes=[pltpu.VMEM((SLABS, SUB), F32)],
        compiler_params=pltpu.CompilerParams(vmem_limit_bytes=12 << 20),
        cost_estimate=pl.CostEstimate(
            flops=2 * SLABS * ORI * SUB, bytes_accessed=3 << 20, transcendentals=0
        ),
        name="pick_rows",
    )(subset, projection)


def expect_kernel(images_ref, volume_ref, picked_ref, precision_ref, partial_ref, evidence_ref):
    images, volume = images_ref[...], volume_ref[...]
    picked = picked_ref[...]
    gram = mm(volume, volume, NT)
    wide = sum(mm(g, picked, NN) for g in parts(gram, 3))
    pfloat = picked.astype(F32)
    energy = jnp.sum(wide * pfloat, axis=0, keepdims=True)
    cross = mm(images, volume, NT)
    correlate = sum(mm(c, picked, NN) for c in parts(cross, 3))
    precision = jnp.transpose(jnp.broadcast_to(precision_ref[...], (128, ROWS)))[:, :1]
    scores = precision * (correlate - 0.5 * energy)
    highest = jnp.max(scores, axis=1, keepdims=True)
    expo = jnp.exp(scores - highest)
    summed = jnp.sum(expo, axis=1, keepdims=True)
    evidence = highest + jnp.log(summed)
    evidence_ref[...] = jnp.transpose(jnp.broadcast_to(evidence, (ROWS, 128)))[:1, :]
    weights = expo * (1.0 / summed)
    occupancy = jnp.sum(weights, axis=0, keepdims=True)
    slab_weight = jnp.sum(occupancy * (pfloat * pfloat), axis=1, keepdims=True)
    mixed = mm(picked, weights.astype(BF16), NT).astype(BF16)
    for c in range(0, FREQ, 512):
        numer = mm(mixed, images_ref[:, c : c + 512], NN)
        partial_ref[:, :, c : c + 512] = numer.astype(BF16).reshape(X * Y, Z, 512)
    lane = lax.broadcasted_iota(jnp.int32, (SLABS, 128), 1)
    high = slab_weight.astype(BF16).astype(F32)
    extra = jnp.where(lane == 0, high, jnp.where(lane == 1, slab_weight - high, 0.0))
    partial_ref[:, :, FREQ:] = extra.astype(BF16).reshape(X * Y, Z, 128)


def expect(images, volume, picked, precision):
    return pl.pallas_call(
        expect_kernel,
        out_shape=(
            jax.ShapeDtypeStruct((X * Y, Z, WIDE), BF16),
            jax.ShapeDtypeStruct((1, ROWS), F32),
        ),
        in_specs=[pl.BlockSpec(memory_space=pltpu.VMEM)] * 4,
        out_specs=[pl.BlockSpec(memory_space=pltpu.VMEM)] * 2,
        compiler_params=pltpu.CompilerParams(vmem_limit_bytes=20 << 20),
        cost_estimate=pl.CostEstimate(
            flops=1400000000, bytes_accessed=4 << 20, transcendentals=ROWS * SUB
        ),
        name="expect",
    )(images, volume, picked, precision)


def gather_slabs(volume):
    column = lax.all_to_all(
        jnp.broadcast_to(volume.reshape(1, 16, 128), (Z, 16, 128)), "z", 0, 0, tiled=True
    )
    column = column.reshape(Z, FREQ)
    whole = lax.all_to_all(
        jnp.broadcast_to(column[None], (X * Y, Z, FREQ)), PLANE, 0, 0, tiled=True
    )
    return whole.reshape(SLABS, FREQ)


def sum_slabs(partial):
    plane = lax.all_to_all(partial, PLANE, 0, 0, tiled=True)
    plane = jnp.sum(plane.astype(F32), axis=0).astype(BF16)
    column = lax.all_to_all(plane.reshape(Z, WIDE // 128, 128), "z", 0, 0, tiled=True)
    return jnp.sum(column.astype(F32), axis=0).reshape(1, WIDE)


def local(images, projection, volume, subset, precision):
    gathered = gather_slabs(volume)
    picked = pick(subset, projection)
    partial, evidence = expect(images, gathered, picked, precision.reshape(1, ROWS))
    mine = sum_slabs(partial)
    weight_mine = mine[:, FREQ : FREQ + 1] + mine[:, FREQ + 1 : FREQ + 2]
    return (mine[:, :FREQ] / (weight_mine + 1.0), evidence.reshape(ROWS))


def solution(mesh):
    grid = Mesh(mesh.devices.reshape(2, X, Y, Z), ("half", "x", "y", "z"))
    every = ("half", "x", "y", "z")
    placed = (P(every, None), P(), P(every, None), P(every, None), P(every))
    return jax.shard_map(
        local,
        mesh=grid,
        in_specs=placed,
        out_specs=(P(every, None), P(every)),
        check_vma=False,
    )
```

time: 107 us -> 98.1 us (0.917)
  matrix products: 10.3 us -> 0 us
  Pallas kernels: 0 us -> 6.42 us
  local copies, waits for them, and re-layouts: 9.58 us -> 4.85 us
  other arithmetic: 4.08 us -> 1.52 us
  waiting for transfers between devices: 10.7 us -> 13.1 us
    dot_general x4 -> x0, matrix products: 10.3 us -> none  [the longest x1 4.73 us: local(): lax.dot_general(picked, backproj, (((0,), (0,)), ((), ())), preferred_ele...]
    pallas_call x0 -> x2, Pallas kernels: none -> 6.42 us  [the longest x1 4.07 us: expect(): pl.pallas_call(expect_kernel, out_shape=(jax.ShapeDtypeStruct((X * Y, Z,...]
    gather x1 -> x0, local copies, waits for them, and re-layouts: 4.94 us -> none  [local(): picked = jnp.take(projection, subset[0], axis=0)]
    unnamed x12 -> x14, local copies, waits for them, and re-layouts: 0.06 us -> 3.11 us
    concatenate x3 -> x0, local copies, waits for them, and re-layouts: 2.81 us -> none  [local(): jnp.concatenate([numerator.astype(jnp.bfloat16), extra], axis=1)]
    all_to_all x1, waiting for transfers between devices: 10.7 us -> 13.1 us  [gather_slabs(): lax.all_to_all(jnp.broadcast_to(column[None], (X * Y, Z, FREQ)), PLANE, 0...]
    reduce_sum x4 -> x2, other arithmetic: 1.87 us -> 0.18 us  [the longest x1 0.15 us: sum_slabs(): plane = jnp.sum(plane.astype(F32), axis=0).astype(BF16)]
  transfers between devices with their start and end apart: 1 -> 1, of which waited for: 1 -> 1; matrix products, arithmetic and copies ran while one was open for 5% -> 0% of each run, Pallas kernels for 0% -> 2%
where the time goes in v2:
time: 98.1 us; the launch traced here: 97.6 us
  blocking collectives  62.5 us (64%)
  waiting for transfers between devices  13.1 us (13%)
  starting transfers between devices  7.17 us (7%)
  Pallas kernels  6.42 us (7%)
  local copies, waits for them, and re-layouts  4.85 us (5%)
  between operations  2.01 us (2%)
  other arithmetic  1.52 us (2%)
    all_to_all x1, blocking collectives, gather_slabs(): lax.all_to_all(jnp.broadcast_to(volume.reshape(1, 16, 128), (Z, 16, 128))...  26.5 us
    all_to_all x1, blocking collectives, sum_slabs(): plane = lax.all_to_all(partial, PLANE, 0, 0, tiled=True)  19.6 us
    all_to_all x1, blocking collectives, sum_slabs(): lax.all_to_all(plane.reshape(Z, WIDE // 128, 128), 'z', 0, 0, tiled=True)  16.4 us
    all_to_all x1, waiting for transfers between devices, gather_slabs(): lax.all_to_all(jnp.broadcast_to(column[None], (X * Y, Z, FREQ)), PLANE, 0...  13.1 us
    all_to_all x1, starting transfers between devices, gather_slabs(): lax.all_to_all(jnp.broadcast_to(column[None], (X * Y, Z, FREQ)), PLANE, 0...  7.17 us
    pallas_call x1, Pallas kernels, expect(): pl.pallas_call(expect_kernel, out_shape=(jax.ShapeDtypeStruct((X * Y, Z,...  4.07 us
    unnamed x14, local copies, waits for them, and re-layouts  3.11 us
    pallas_call x1, Pallas kernels, pick(): pl.pallas_call(pick_kernel, out_shape=jax.ShapeDtypeStruct((SLABS, SUB),...  2.34 us
  transfers between devices with their start and end apart: 1, of which 1 were waited for; matrix products, arithmetic and copies ran while one was open for 0% of the time, Pallas kernels for 2%

profile of v2, /device:TPU:32, one launch (start us, length us, event | category | flops | bytes accessed | tf_op | source)
XLA Modules:
  0.0 97.6 jit_solution(3633130759650499434)
XLA Ops:
  0.6 0.7 reduce.1
  1.4 26.5 %all_to_all.20 = bf16[16,16,128]{2,1,0:T(8,128)(2,1)S(1)} all-to-all(bf16[16,16,128]{2,1,0:T(8,128)(2,1)S(1)} %broadcast_in_dim.15), channel_id=1, replica_groups=mesh['half'=2,'x'=4,'y'=4,'z'=16] {'z'}, dimensions={0} | all-to-all | bytes 131072 | tf_op jit(solution)/shard_map/all_to_all | solution.py:108
  27.9 0.0 copy-start.2
  27.9 1.1 %broadcast_in_dim.17 = bf16[16,16,2048]{2,1,0:T(8,128)(2,1)} broadcast(bf16[16,2048]{1,0:T(8,128)(2,1)S(1)} %bitcast.16), dimensions={1,2} | broadcast | bytes 1114112 | tf_op jit(solution)/shard_map/broadcast_in_dim | solution.py:113
  29.0 0.0 copy-start
  29.0 7.2 %all-to-all-start.1 = ((bf16[16,16,2048]{2,1,0:T(8,128)(2,1)}), bf16[16,16,2048]{2,1,0:T(8,128)(2,1)S(1)}, u32[]{:S(2)}, u32[]{:S(2)}) async-start(bf16[16,16,2048]{2,1,0:T(8,128)(2,1)} %broadcast_in_dim.17), calls=%async_computation.1 | async-start | bytes 2097152 | tf_op jit(solution)/shard_map/all_to_all | solution.py:112
  36.2 0.0 copy-done.2
  36.2 0.0 copy-done
  36.2 0.0 copy-start.3
  36.3 2.3 %pick_rows.1.picked_ref = bf16[256,1024]{1,0:T(8,128)(2,1)S(1)} custom-call(s32[1,1024]{1,0:T(1,128)S(1)} %copy-done.2, bf16[4096,256]{1,0:T(8,128)(2,1)S(1)} %copy-done), custom_call_target="tpu_custom_call" | custom-call | flops 2147483648 | bytes 3145728 | tf_op jit(solution)/shard_map/pick_rows/pallas_call | solution.py:47
  38.6 0.0 copy-start.4
  38.6 0.8 copy-done.4
  39.4 13.1 %all-to-all-done.1 = bf16[16,16,2048]{2,1,0:T(8,128)(2,1)S(1)} async-done(((bf16[16,16,2048]{2,1,0:T(8,128)(2,1)}), bf16[16,16,2048]{2,1,0:T(8,128)(2,1)S(1)}, u32[]{:S(2)}, u32[]{:S(2)}) %all-to-all-start.1) | async-done | bytes 1048608 | tf_op jit(solution)/shard_map/all_to_all | solution.py:112
  52.6 0.0 copy-done.3
  52.6 0.0 copy-start.1
  52.6 1.2 %copy-done.1 = bf16[256,2048]{1,0:T(8,128)(2,1)S(1)} copy-done((bf16[256,2048]{1,0:T(8,128)(2,1)S(1)}, bf16[256,2048]{1,0:T(8,128)(2,1)}, u32[]{:S(2)}) %copy-start.1) | copy-done | bytes 1048600
  53.8 0.0 copy-start.5
  53.8 1.0 %copy-done.5 = bf16[256,1024]{1,0:T(8,128)(2,1)S(1)} copy-done((bf16[256,1024]{1,0:T(8,128)(2,1)S(1)}, bf16[256,1024]{1,0:T(8,128)(2,1)}, u32[]{:S(2)}) %copy-start.5) | copy-done | bytes 524312
  54.8 4.1 %expect.1 = (bf16[16,16,2176]{2,1,0:T(8,128)(2,1)S(1)}, f32[1,256]{1,0:T(1,128)}) custom-call(bf16[256,2048]{1,0:T(8,128)(2,1)S(1)} %copy-done.1, bf16[256,2048]{1,0:T(8,128)(2,1)S(1)} %bitcast.14, bf16[256,1024]{1,0:T(8,128)(2,1)S(1)} %copy-done.5, f32[1,256]{1,0:T(1,128)S(1)} %bitcast.15), custom_call_target="tpu_custom_call" | custom-call | flops 1400000000 | bytes 4194304 | tf_op jit(solution)/shard_map/expect/pallas_call | solution.py:91
  58.9 19.6 %all_to_all.21 = bf16[16,16,2176]{2,1,0:T(8,128)(2,1)S(1)} all-to-all(bf16[16,16,2176]{2,1,0:T(8,128)(2,1)S(1)} %get-tuple-element.4), channel_id=1, replica_groups=mesh['half'=2,'x'=4,'y'=4,'z'=16] {'x','y'}, dimensions={0} | all-to-all | bytes 2228224 | tf_op jit(solution)/shard_map/all_to_all | solution.py:119
  78.5 0.2 reduce_sum.21
  78.7 16.4 %all_to_all.22 = bf16[16,17,128]{2,1,0:T(8,128)(2,1)S(1)} all-to-all(bf16[16,17,128]{2,1,0:T(8,128)(2,1)S(1)} %reshape.26), channel_id=1, replica_groups=mesh['half'=2,'x'=4,'y'=4,'z'=16] {'z'}, dimensions={0} | all-to-all | bytes 139264 | tf_op jit(solution)/shard_map/all_to_all | solution.py:121
  95.1 0.6 fusion
  97.0 0.6 slice_divide_fusion
  (5 shorter events, 0.1 us)
Async XLA Ops:
  27.9 8.3 %copy-start.2 = (s32[1,1024]{1,0:T(1,128)S(1)}, s32[1,1024]{1,0:T(1,128)}, u32[]{:S(2)}) copy-start(s32[1,1024]{1,0:T(1,128)} %subset_ref.1) | copy-start | bytes 12292
  29.0 7.2 %copy-start = (bf16[4096,256]{1,0:T(8,128)(2,1)S(1)}, bf16[4096,256]{1,0:T(8,128)(2,1)}, u32[]{:S(2)}) copy-start(bf16[4096,256]{1,0:T(8,128)(2,1)} %projection_ref.1) | copy-start | bytes 6291460
  29.0 23.5 %all-to-all-start.1 = ((bf16[16,16,2048]{2,1,0:T(8,128)(2,1)}), bf16[16,16,2048]{2,1,0:T(8,128)(2,1)S(1)}, u32[]{:S(2)}, u32[]{:S(2)}) async-start(bf16[16,16,2048]{2,1,0:T(8,128)(2,1)} %broadcast_in_dim.17), calls=%async_computation.1 | async-start | bytes 2097152 | tf_op jit(solution)/shard_map/all_to_all | solution.py:112
  36.2 16.3 %copy-start.3 = (f32[256]{0:T(256)S(1)}, f32[256]{0:T(256)}, u32[]{:S(2)}) copy-start(f32[256]{0:T(256)} %param.9) | copy-start | bytes 3076
  38.6 0.8 copy-start.4
  52.6 1.2 %copy-start.1 = (bf16[256,2048]{1,0:T(8,128)(2,1)S(1)}, bf16[256,2048]{1,0:T(8,128)(2,1)}, u32[]{:S(2)}) copy-start(bf16[256,2048]{1,0:T(8,128)(2,1)} %images_ref.1) | copy-start | bytes 3145732
  53.8 1.0 %copy-start.5 = (bf16[256,1024]{1,0:T(8,128)(2,1)S(1)}, bf16[256,1024]{1,0:T(8,128)(2,1)}, u32[]{:S(2)}) copy-start(bf16[256,1024]{1,0:T(8,128)(2,1)} %copy-done.4) | copy-start | bytes 1572868

commit v3 on v2

--- a/solution.py
+++ b/solution.py
@@ -104,31 +104,42 @@
     )(images, volume, picked, precision)
 
 
-def gather_slabs(volume):
+def gather_slabs(volume, picked):
     column = lax.all_to_all(
         jnp.broadcast_to(volume.reshape(1, 16, 128), (Z, 16, 128)), "z", 0, 0, tiled=True
     )
-    column = column.reshape(Z, FREQ)
+    column, picked = lax.optimization_barrier((column.reshape(Z, FREQ), picked))
     whole = lax.all_to_all(
         jnp.broadcast_to(column[None], (X * Y, Z, FREQ)), PLANE, 0, 0, tiled=True
     )
-    return whole.reshape(SLABS, FREQ)
+    return whole.reshape(SLABS, FREQ), picked
 
 
-def sum_slabs(partial):
+def finish_kernel(column_ref, new_ref):
+    total = jnp.sum(column_ref[...].astype(F32), axis=0)
+    weight = total[FREQ // 128 :, :1] + total[FREQ // 128 :, 1:2]
+    new_ref[...] = total[: FREQ // 128, :] / (weight + 1.0)
+
+
+def new_slab(partial):
     plane = lax.all_to_all(partial, PLANE, 0, 0, tiled=True)
     plane = jnp.sum(plane.astype(F32), axis=0).astype(BF16)
     column = lax.all_to_all(plane.reshape(Z, WIDE // 128, 128), "z", 0, 0, tiled=True)
-    return jnp.sum(column.astype(F32), axis=0).reshape(1, WIDE)
+    return pl.pallas_call(
+        finish_kernel,
+        out_shape=jax.ShapeDtypeStruct((FREQ // 128, 128), F32),
+        in_specs=[pl.BlockSpec(memory_space=pltpu.VMEM)],
+        out_specs=pl.BlockSpec(memory_space=pltpu.VMEM),
+        compiler_params=pltpu.CompilerParams(vmem_limit_bytes=8 << 20),
+        cost_estimate=pl.CostEstimate(flops=100000, bytes_accessed=1 << 17, transcendentals=0),
+        name="finish",
+    )(column).reshape(1, FREQ)
 
 
 def local(images, projection, volume, subset, precision):
-    gathered = gather_slabs(volume)
-    picked = pick(subset, projection)
+    gathered, picked = gather_slabs(volume, pick(subset, projection))
     partial, evidence = expect(images, gathered, picked, precision.reshape(1, ROWS))
-    mine = sum_slabs(partial)
-    weight_mine = mine[:, FREQ : FREQ + 1] + mine[:, FREQ + 1 : FREQ + 2]
-    return (mine[:, :FREQ] / (weight_mine + 1.0), evidence.reshape(ROWS))
+    return (new_slab(partial), evidence.reshape(ROWS))
 
 
 def solution(mesh):

time: 98.1 us -> 94.4 us (0.962)
  starting transfers between devices: 7.17 us -> 15.2 us
  waiting for transfers between devices: 13.1 us -> 6.91 us
  blocking collectives: 62.5 us -> 60.1 us
  local copies, waits for them, and re-layouts: 4.85 us -> 3.08 us
  between operations: 2.01 us -> 0.68 us
    all_to_all x1, starting transfers between devices: 7.17 us -> 15.2 us  [gather_slabs(): lax.all_to_all(jnp.broadcast_to(volume.reshape(1, 16, 128), (Z, 16, 128))...]
    all_to_all x1, waiting for transfers between devices: 13.1 us -> 6.91 us  [gather_slabs(): lax.all_to_all(jnp.broadcast_to(volume.reshape(1, 16, 128), (Z, 16, 128))...]
    all_to_all x3, blocking collectives: 62.5 us -> 60.1 us  [the longest x1 23.2 us: gather_slabs(): lax.all_to_all(jnp.broadcast_to(column[None], (X * Y, Z, FREQ)), PLANE, 0...]
    broadcast_in_dim x1, local copies, waits for them, and re-layouts: 1.1 us -> 0.11 us  [gather_slabs(): jnp.broadcast_to(column[None], (X * Y, Z, FREQ))]
    unnamed x14 -> x9, local copies, waits for them, and re-layouts: 3.11 us -> 2.3 us
where the time goes in v3:
time: 94.4 us; the launch traced here: 94 us
  blocking collectives  60.1 us (64%)
  starting transfers between devices  15.2 us (16%)
  Pallas kernels  7.14 us (8%)
  waiting for transfers between devices  6.91 us (7%)
  local copies, waits for them, and re-layouts  3.08 us (3%)
    all_to_all x1, blocking collectives, gather_slabs(): lax.all_to_all(jnp.broadcast_to(column[None], (X * Y, Z, FREQ)), PLANE, 0...  23.2 us
    all_to_all x1, blocking collectives, new_slab(): plane = lax.all_to_all(partial, PLANE, 0, 0, tiled=True)  19 us
    all_to_all x1, blocking collectives, new_slab(): lax.all_to_all(plane.reshape(Z, WIDE // 128, 128), 'z', 0, 0, tiled=True)  17.8 us
    all_to_all x1, starting transfers between devices, gather_slabs(): lax.all_to_all(jnp.broadcast_to(volume.reshape(1, 16, 128), (Z, 16, 128))...  15.2 us
    all_to_all x1, waiting for transfers between devices, gather_slabs(): lax.all_to_all(jnp.broadcast_to(volume.reshape(1, 16, 128), (Z, 16, 128))...  6.91 us
    pallas_call x1, Pallas kernels, expect(): pl.pallas_call(expect_kernel, out_shape=(jax.ShapeDtypeStruct((X * Y, Z,...  4.07 us
    pallas_call x1, Pallas kernels, pick(): pl.pallas_call(pick_kernel, out_shape=jax.ShapeDtypeStruct((SLABS, SUB),...  2.34 us
    unnamed x9, local copies, waits for them, and re-layouts  2.3 us
  transfers between devices with their start and end apart: 1, of which 1 were waited for; matrix products, arithmetic and copies ran while one was open for 0% of the time, Pallas kernels for 2%

profile of v3, /device:TPU:32, one launch (start us, length us, event | category | flops | bytes accessed | tf_op | source)
XLA Modules:
  0.0 94.0 jit_solution(13412336879171987521)
XLA Ops:
  0.6 0.7 reduce.1
  1.4 0.6 broadcast_in_dim.14
  2.0 15.2 %all-to-all-start = ((bf16[16,16,128]{2,1,0:T(8,128)(2,1)}), bf16[16,16,128]{2,1,0:T(8,128)(2,1)S(1)}, u32[]{:S(2)}, u32[]{:S(2)}) async-start(bf16[16,16,128]{2,1,0:T(8,128)(2,1)} %broadcast_in_dim.14), calls=%async_computation | async-start | bytes 131072 | tf_op jit(solution)/shard_map/all_to_all | solution.py:108
  17.2 0.0 copy-start
  17.2 1.6 %copy-done = bf16[4096,256]{1,0:T(8,128)(2,1)S(1)} copy-done((bf16[4096,256]{1,0:T(8,128)(2,1)S(1)}, bf16[4096,256]{1,0:T(8,128)(2,1)}, u32[]{:S(2)}) %copy-start) | copy-done | bytes 2097176
  18.8 0.0 copy-start.2
  18.8 0.7 copy-done.2
  19.5 2.3 %pick_rows.1.picked_ref = bf16[256,1024]{1,0:T(8,128)(2,1)S(1)} custom-call(s32[1,1024]{1,0:T(1,128)S(1)} %copy-done.2, bf16[4096,256]{1,0:T(8,128)(2,1)S(1)} %copy-done), custom_call_target="tpu_custom_call" | custom-call | flops 2147483648 | bytes 3145728 | tf_op jit(solution)/shard_map/pick_rows/pallas_call | solution.py:47
  21.8 6.9 %all-to-all-done = bf16[16,16,128]{2,1,0:T(8,128)(2,1)S(1)} async-done(((bf16[16,16,128]{2,1,0:T(8,128)(2,1)}), bf16[16,16,128]{2,1,0:T(8,128)(2,1)S(1)}, u32[]{:S(2)}, u32[]{:S(2)}) %all-to-all-start) | async-done | bytes 65568 | tf_op jit(solution)/shard_map/all_to_all | solution.py:108
  28.7 0.1 broadcast_in_dim.15
  28.9 0.0 copy-start.1
  28.9 0.0 copy-start.3
  28.9 23.2 %all_to_all.20 = bf16[16,16,2048]{2,1,0:T(8,128)(2,1)S(1)} all-to-all(bf16[16,16,2048]{2,1,0:T(8,128)(2,1)S(1)} %broadcast_in_dim.15), channel_id=1, replica_groups=mesh['half'=2,'x'=4,'y'=4,'z'=16] {'x','y'}, dimensions={0} | all-to-all | bytes 2097152 | tf_op jit(solution)/shard_map/all_to_all | solution.py:112
  52.1 0.0 copy-done.1
  52.1 0.0 copy-done.3
  52.1 4.1 %expect.1 = (bf16[16,16,2176]{2,1,0:T(8,128)(2,1)S(1)}, f32[1,256]{1,0:T(1,128)}) custom-call(bf16[256,2048]{1,0:T(8,128)(2,1)S(1)} %copy-done.1, bf16[256,2048]{1,0:T(8,128)(2,1)S(1)} %bitcast.9, bf16[256,1024]{1,0:T(8,128)(2,1)S(1)} %pick_rows.1.picked_ref, f32[1,256]{1,0:T(1,128)S(1)} %bitcast.10), custom_call_target="tpu_custom_call" | custom-call | flops 1400000000 | bytes 4194304 | tf_op jit(solution)/shard_map/expect/pallas_call | solution.py:91
  56.2 19.0 %all_to_all.21 = bf16[16,16,2176]{2,1,0:T(8,128)(2,1)S(1)} all-to-all(bf16[16,16,2176]{2,1,0:T(8,128)(2,1)S(1)} %get-tuple-element.8), channel_id=1, replica_groups=mesh['half'=2,'x'=4,'y'=4,'z'=16] {'x','y'}, dimensions={0} | all-to-all | bytes 2228224 | tf_op jit(solution)/shard_map/all_to_all | solution.py:125
  75.2 0.2 reduce_sum.12
  75.4 17.8 %all_to_all.22.column_ref = bf16[16,17,128]{2,1,0:T(8,128)(2,1)S(1)} all-to-all(bf16[16,17,128]{2,1,0:T(8,128)(2,1)S(1)} %reshape.28), channel_id=1, replica_groups=mesh['half'=2,'x'=4,'y'=4,'z'=16] {'z'}, dimensions={0} | all-to-all | bytes 139264 | tf_op jit(solution)/shard_map/all_to_all | solution.py:127
  93.3 0.7 finish.1
  (2 shorter events, 0.1 us)
Async XLA Ops:
  2.0 26.7 %all-to-all-start = ((bf16[16,16,128]{2,1,0:T(8,128)(2,1)}), bf16[16,16,128]{2,1,0:T(8,128)(2,1)S(1)}, u32[]{:S(2)}, u32[]{:S(2)}) async-start(bf16[16,16,128]{2,1,0:T(8,128)(2,1)} %broadcast_in_dim.14), calls=%async_computation | async-start | bytes 131072 | tf_op jit(solution)/shard_map/all_to_all | solution.py:108
  17.2 1.6 %copy-start = (bf16[4096,256]{1,0:T(8,128)(2,1)S(1)}, bf16[4096,256]{1,0:T(8,128)(2,1)}, u32[]{:S(2)}) copy-start(bf16[4096,256]{1,0:T(8,128)(2,1)} %projection_ref.1) | copy-start | bytes 6291460
  18.8 0.7 copy-start.2
  28.9 23.3 %copy-start.1 = (bf16[256,2048]{1,0:T(8,128)(2,1)S(1)}, bf16[256,2048]{1,0:T(8,128)(2,1)}, u32[]{:S(2)}) copy-start(bf16[256,2048]{1,0:T(8,128)(2,1)} %images_ref.1) | copy-start | bytes 3145732
  28.9 23.2 %copy-start.3 = (f32[256]{0:T(256)S(1)}, f32[256]{0:T(256)}, u32[]{:S(2)}) copy-start(f32[256]{0:T(256)} %param.9) | copy-start | bytes 3076

commit v4 on v3

--- a/solution.py
+++ b/solution.py
@@ -27,35 +27,75 @@
     return found
 
 
-def pick_kernel(subset_ref, projection_ref, picked_ref, total_ref):
+BLOCKS = 2
+BLOCK = ORI // BLOCKS
+
+
+def pick_rows(
+    subset_hbm, projection_hbm, out_hbm, subset_ref, rows_ref, total_ref, picked_ref, sems
+):
+    subset_copy = pltpu.make_async_copy(subset_hbm, subset_ref, sems.at[BLOCKS])
+    subset_copy.start()
+    copies = []
+    for b in range(BLOCKS):
+        here = pl.ds(b * BLOCK, BLOCK)
+        copies.append(
+            pltpu.make_async_copy(projection_hbm.at[here], rows_ref.at[here], sems.at[b])
+        )
+        copies[-1].start()
+    rows = lax.broadcasted_iota(jnp.int32, (256, SUB), 0).astype(F32).astype(BF16)
+    subset_copy.wait()
     subset = subset_ref[...]
     block = subset // 256
     within = subset - block * 256
-    rows = lax.broadcasted_iota(jnp.int32, (256, SUB), 0).astype(F32).astype(BF16)
     for k in range(ORI // 256):
         wanted = jnp.where(block == k, within, -1).astype(F32).astype(BF16)
         chosen = jnp.where(rows == wanted, jnp.ones((), BF16), jnp.zeros((), BF16))
-        part = mm(projection_ref[k * 256 : (k + 1) * 256, :], chosen, TN)
+        if k * 256 % BLOCK == 0:
+            copies[k * 256 // BLOCK].wait()
+        part = mm(rows_ref[k * 256 : (k + 1) * 256, :], chosen, TN)
         if k == 0:
             total_ref[...] = part
         else:
             total_ref[...] += part
     picked_ref[...] = total_ref[...].astype(BF16)
+    out = pltpu.make_async_copy(picked_ref, out_hbm, sems.at[BLOCKS])
+    out.start()
+    out.wait()
 
 
-def pick(subset, projection):
+def pick_first_kernel(subset_hbm, projection_hbm, *refs):
+    @pl.when(lax.axis_index("half") == 0)
+    def _():
+        pick_rows(subset_hbm, projection_hbm, *refs)
+
+
+def pick_second_kernel(subset_hbm, projection_hbm, held_ref, *refs):
+    @pl.when(lax.axis_index("half") == 1)
+    def _():
+        pick_rows(subset_hbm, projection_hbm, *refs)
+
+
+def pick(kernel, name, subset, projection, *held):
     return pl.pallas_call(
-        pick_kernel,
+        kernel,
         out_shape=jax.ShapeDtypeStruct((SLABS, SUB), BF16),
-        in_specs=[pl.BlockSpec(memory_space=pltpu.VMEM)] * 2,
-        out_specs=pl.BlockSpec(memory_space=pltpu.VMEM),
-        scratch_shapes=[pltpu.VMEM((SLABS, SUB), F32)],
-        compiler_params=pltpu.CompilerParams(vmem_limit_bytes=12 << 20),
+        in_specs=[pl.BlockSpec(memory_space=pltpu.HBM)] * (2 + len(held)),
+        out_specs=pl.BlockSpec(memory_space=pltpu.HBM),
+        input_output_aliases={2: 0} if held else {},
+        scratch_shapes=[
+            pltpu.VMEM((1, SUB), jnp.int32),
+            pltpu.VMEM((ORI, SLABS), BF16),
+            pltpu.VMEM((SLABS, SUB), F32),
+            pltpu.VMEM((SLABS, SUB), BF16),
+            pltpu.SemaphoreType.DMA((BLOCKS + 1,)),
+        ],
+        compiler_params=pltpu.CompilerParams(vmem_limit_bytes=60 << 20),
         cost_estimate=pl.CostEstimate(
             flops=2 * SLABS * ORI * SUB, bytes_accessed=3 << 20, transcendentals=0
         ),
-        name="pick_rows",
-    )(subset, projection)
+        name=name,
+    )(subset, projection, *held)
 
 
 def expect_kernel(images_ref, volume_ref, picked_ref, precision_ref, partial_ref, evidence_ref):
@@ -104,10 +144,13 @@
     )(images, volume, picked, precision)
 
 
-def gather_slabs(volume, picked):
+def gather_slabs(volume, subset, projection):
+    picked = pick(pick_first_kernel, "pick_first", subset, projection)
+    volume, picked = lax.optimization_barrier((volume, picked))
     column = lax.all_to_all(
         jnp.broadcast_to(volume.reshape(1, 16, 128), (Z, 16, 128)), "z", 0, 0, tiled=True
     )
+    picked = pick(pick_second_kernel, "pick_second", subset, projection, picked)
     column, picked = lax.optimization_barrier((column.reshape(Z, FREQ), picked))
     whole = lax.all_to_all(
         jnp.broadcast_to(column[None], (X * Y, Z, FREQ)), PLANE, 0, 0, tiled=True
@@ -137,7 +180,7 @@
 
 
 def local(images, projection, volume, subset, precision):
-    gathered, picked = gather_slabs(volume, pick(subset, projection))
+    gathered, picked = gather_slabs(volume, subset, projection)
     partial, evidence = expect(images, gathered, picked, precision.reshape(1, ROWS))
     return (new_slab(partial), evidence.reshape(ROWS))
 

time: 94.4 us -> 91.3 us (0.967)
  blocking collectives: 60.1 us -> 53 us
  waiting for transfers between devices: 6.91 us -> 11.8 us
  local copies, waits for them, and re-layouts: 3.08 us -> 0.82 us
  Pallas kernels: 7.14 us -> 9.32 us
    all_to_all x1, waiting for transfers between devices: 6.91 us -> 11.8 us  [gather_slabs(): lax.all_to_all(jnp.broadcast_to(volume.reshape(1, 16, 128), (Z, 16, 128))...]
    all_to_all x1, blocking collectives: 23.2 us -> 19.9 us  [gather_slabs(): lax.all_to_all(jnp.broadcast_to(column[None], (X * Y, Z, FREQ)), PLANE, 0...]
    all_to_all x1, blocking collectives: 19 us -> 16.5 us  [new_slab(): plane = lax.all_to_all(partial, PLANE, 0, 0, tiled=True)]
    unnamed x9, local copies, waits for them, and re-layouts: 2.3 us -> 0.04 us
    pallas_call x1 -> x2, Pallas kernels: 2.34 us -> 4.5 us  [pick(): pl.pallas_call(kernel, out_shape=jax.ShapeDtypeStruct((SLABS, SUB), BF16)...]
    all_to_all x1, blocking collectives: 17.8 us -> 16.6 us  [new_slab(): lax.all_to_all(plane.reshape(Z, WIDE // 128, 128), 'z', 0, 0, tiled=True)]
  transfers between devices with their start and end apart: 1 -> 1, of which waited for: 1 -> 1; matrix products, arithmetic and copies ran while one was open for 0% -> 0% of each run, Pallas kernels for 2% -> 0%
where the time goes in v4:
time: 91.3 us; the launch traced here: 91 us
  blocking collectives  53 us (58%)
  starting transfers between devices  15.2 us (17%)
  waiting for transfers between devices  11.8 us (13%)
  Pallas kernels  9.32 us (10%)
    all_to_all x1, blocking collectives, gather_slabs(): lax.all_to_all(jnp.broadcast_to(column[None], (X * Y, Z, FREQ)), PLANE, 0...  19.9 us
    all_to_all x1, blocking collectives, new_slab(): lax.all_to_all(plane.reshape(Z, WIDE // 128, 128), 'z', 0, 0, tiled=True)  16.6 us
    all_to_all x1, blocking collectives, new_slab(): plane = lax.all_to_all(partial, PLANE, 0, 0, tiled=True)  16.5 us
    all_to_all x1, starting transfers between devices, gather_slabs(): lax.all_to_all(jnp.broadcast_to(volume.reshape(1, 16, 128), (Z, 16, 128))...  15.2 us
    all_to_all x1, waiting for transfers between devices, gather_slabs(): lax.all_to_all(jnp.broadcast_to(volume.reshape(1, 16, 128), (Z, 16, 128))...  11.8 us
    pallas_call x2, Pallas kernels, pick(): pl.pallas_call(kernel, out_shape=jax.ShapeDtypeStruct((SLABS, SUB), BF16)...  4.5 us
    pallas_call x1, Pallas kernels, expect(): pl.pallas_call(expect_kernel, out_shape=(jax.ShapeDtypeStruct((X * Y, Z,...  4.08 us
  transfers between devices with their start and end apart: 1, of which 1 were waited for; matrix products, arithmetic and copies ran while one was open for 0% of the time, Pallas kernels for 0%

profile of v4, /device:TPU:32, one launch (start us, length us, event | category | flops | bytes accessed | tf_op | source)
XLA Modules:
  0.0 91.0 jit_solution(799364322052266030)
XLA Ops:
  0.6 0.0 copy-start.3
  0.6 4.5 %pick_first.1.held_ref = bf16[256,1024]{1,0:T(8,128)(2,1)} custom-call(s32[1,1024]{1,0:T(1,128)} %subset_hbm.3, bf16[4096,256]{1,0:T(8,128)(2,1)} %projection_hbm.3), custom_call_target="tpu_custom_call" | custom-call | flops 2147483648 | bytes 3145728 | tf_op jit(solution)/shard_map/pick_first/pallas_call | solution.py:80
  5.1 0.0 copy-done.3
  5.2 0.6 broadcast_in_dim.14
  5.8 15.2 %all-to-all-start = ((bf16[16,16,128]{2,1,0:T(8,128)(2,1)}), bf16[16,16,128]{2,1,0:T(8,128)(2,1)S(1)}, u32[]{:S(2)}, u32[]{:S(2)}) async-start(bf16[16,16,128]{2,1,0:T(8,128)(2,1)} %broadcast_in_dim.14), calls=%async_computation | async-start | bytes 131072 | tf_op jit(solution)/shard_map/all_to_all | solution.py:150
  21.0 11.8 %all-to-all-done = bf16[16,16,128]{2,1,0:T(8,128)(2,1)S(1)} async-done(((bf16[16,16,128]{2,1,0:T(8,128)(2,1)}), bf16[16,16,128]{2,1,0:T(8,128)(2,1)S(1)}, u32[]{:S(2)}, u32[]{:S(2)}) %all-to-all-start) | async-done | bytes 65568 | tf_op jit(solution)/shard_map/all_to_all | solution.py:150
  32.9 0.1 broadcast_in_dim.15
  33.0 0.0 copy-start
  33.0 0.0 copy-start.1
  33.0 0.0 copy-start.2
  33.0 19.9 %all_to_all.20 = bf16[16,16,2048]{2,1,0:T(8,128)(2,1)S(1)} all-to-all(bf16[16,16,2048]{2,1,0:T(8,128)(2,1)S(1)} %broadcast_in_dim.15), channel_id=1, replica_groups=mesh['half'=2,'x'=4,'y'=4,'z'=16] {'x','y'}, dimensions={0} | all-to-all | bytes 2097152 | tf_op jit(solution)/shard_map/all_to_all | solution.py:155
  52.9 0.0 copy-done
  52.9 0.0 copy-done.1
  52.9 0.0 copy-done.2
  52.9 4.1 %expect.1 = (bf16[16,16,2176]{2,1,0:T(8,128)(2,1)S(1)}, f32[1,256]{1,0:T(1,128)}) custom-call(bf16[256,2048]{1,0:T(8,128)(2,1)S(1)} %copy-done, bf16[256,2048]{1,0:T(8,128)(2,1)S(1)} %bitcast.9, bf16[256,1024]{1,0:T(8,128)(2,1)S(1)} %copy-done.2, f32[1,256]{1,0:T(1,128)S(1)} %bitcast.10), custom_call_target="tpu_custom_call" | custom-call | flops 1400000000 | bytes 4194304 | tf_op jit(solution)/shard_map/expect/pallas_call | solution.py:131
  57.0 16.5 %all_to_all.21 = bf16[16,16,2176]{2,1,0:T(8,128)(2,1)S(1)} all-to-all(bf16[16,16,2176]{2,1,0:T(8,128)(2,1)S(1)} %get-tuple-element.12), channel_id=1, replica_groups=mesh['half'=2,'x'=4,'y'=4,'z'=16] {'x','y'}, dimensions={0} | all-to-all | bytes 2228224 | tf_op jit(solution)/shard_map/all_to_all | solution.py:168
  73.5 0.2 reduce_sum.12
  73.7 16.6 %all_to_all.22.column_ref = bf16[16,17,128]{2,1,0:T(8,128)(2,1)S(1)} all-to-all(bf16[16,17,128]{2,1,0:T(8,128)(2,1)S(1)} %reshape.28), channel_id=1, replica_groups=mesh['half'=2,'x'=4,'y'=4,'z'=16] {'z'}, dimensions={0} | all-to-all | bytes 139264 | tf_op jit(solution)/shard_map/all_to_all | solution.py:170
  90.3 0.7 finish.1
  (4 shorter events, 0.1 us)
Async XLA Ops:
  0.6 4.5 %copy-start.3 = (bf16[1,2048]{1,0:T(2,128)(2,1)S(1)}, bf16[1,2048]{1,0:T(2,128)(2,1)}, u32[]{:S(2)}) copy-start(bf16[1,2048]{1,0:T(2,128)(2,1)} %param.7) | copy-start | bytes 12292
  5.8 27.0 %all-to-all-start = ((bf16[16,16,128]{2,1,0:T(8,128)(2,1)}), bf16[16,16,128]{2,1,0:T(8,128)(2,1)S(1)}, u32[]{:S(2)}, u32[]{:S(2)}) async-start(bf16[16,16,128]{2,1,0:T(8,128)(2,1)} %broadcast_in_dim.14), calls=%async_computation | async-start | bytes 131072 | tf_op jit(solution)/shard_map/all_to_all | solution.py:150
  33.0 19.9 %copy-start = (bf16[256,2048]{1,0:T(8,128)(2,1)S(1)}, bf16[256,2048]{1,0:T(8,128)(2,1)}, u32[]{:S(2)}) copy-start(bf16[256,2048]{1,0:T(8,128)(2,1)} %images_ref.1) | copy-start | bytes 3145732
  33.0 19.9 %copy-start.1 = (f32[256]{0:T(256)S(1)}, f32[256]{0:T(256)}, u32[]{:S(2)}) copy-start(f32[256]{0:T(256)} %param.9) | copy-start | bytes 3076
  33.0 19.9 %copy-start.2 = (bf16[256,1024]{1,0:T(8,128)(2,1)S(1)}, bf16[256,1024]{1,0:T(8,128)(2,1)}, u32[]{:S(2)}) copy-start(bf16[256,1024]{1,0:T(8,128)(2,1)} %pick_second.1.picked_ref) | copy-start | bytes 1572868

commit v5 on v4

--- a/solution.py
+++ b/solution.py
@@ -102,11 +102,12 @@
     images, volume = images_ref[...], volume_ref[...]
     picked = picked_ref[...]
     gram = mm(volume, volume, NT)
-    wide = sum(mm(g, picked, NN) for g in parts(gram, 3))
+    cross = mm(images, volume, NT)
+    many = mm(jnp.concatenate(parts(gram, 3) + parts(cross, 3), axis=0), picked, NN)
+    wide = sum(many[k * SLABS : (k + 1) * SLABS] for k in range(3))
+    correlate = sum(many[k * ROWS : (k + 1) * ROWS] for k in range(3, 6))
     pfloat = picked.astype(F32)
     energy = jnp.sum(wide * pfloat, axis=0, keepdims=True)
-    cross = mm(images, volume, NT)
-    correlate = sum(mm(c, picked, NN) for c in parts(cross, 3))
     precision = jnp.transpose(jnp.broadcast_to(precision_ref[...], (128, ROWS)))[:, :1]
     scores = precision * (correlate - 0.5 * energy)
     highest = jnp.max(scores, axis=1, keepdims=True)

time: 91.3 us -> 90.6 us (level)
  no operation moved by 1% of the time
where the time goes in v5:
time: 90.6 us; the launch traced here: 90.3 us
  blocking collectives  53 us (58%)
  starting transfers between devices  15.2 us (17%)
  waiting for transfers between devices  11.8 us (13%)
  Pallas kernels  8.55 us (9%)
    all_to_all x1, blocking collectives, gather_slabs(): lax.all_to_all(jnp.broadcast_to(column[None], (X * Y, Z, FREQ)), PLANE, 0...  19.9 us
    all_to_all x1, blocking collectives, new_slab(): lax.all_to_all(plane.reshape(Z, WIDE // 128, 128), 'z', 0, 0, tiled=True)  16.6 us
    all_to_all x1, blocking collectives, new_slab(): plane = lax.all_to_all(partial, PLANE, 0, 0, tiled=True)  16.5 us
    all_to_all x1, starting transfers between devices, gather_slabs(): lax.all_to_all(jnp.broadcast_to(volume.reshape(1, 16, 128), (Z, 16, 128))...  15.2 us
    all_to_all x1, waiting for transfers between devices, gather_slabs(): lax.all_to_all(jnp.broadcast_to(volume.reshape(1, 16, 128), (Z, 16, 128))...  11.8 us
    pallas_call x2, Pallas kernels, pick(): pl.pallas_call(kernel, out_shape=jax.ShapeDtypeStruct((SLABS, SUB), BF16)...  4.5 us
    pallas_call x1, Pallas kernels, expect(): pl.pallas_call(expect_kernel, out_shape=(jax.ShapeDtypeStruct((X * Y, Z,...  3.32 us
  transfers between devices with their start and end apart: 1, of which 1 were waited for; matrix products, arithmetic and copies ran while one was open for 0% of the time, Pallas kernels for 0%

profile of v5, /device:TPU:32, one launch (start us, length us, event | category | flops | bytes accessed | tf_op | source)
XLA Modules:
  0.0 90.3 jit_solution(10421034510085523579)
XLA Ops:
  0.6 0.0 copy-start.3
  0.6 4.5 %pick_first.1.held_ref = bf16[256,1024]{1,0:T(8,128)(2,1)} custom-call(s32[1,1024]{1,0:T(1,128)} %subset_hbm.3, bf16[4096,256]{1,0:T(8,128)(2,1)} %projection_hbm.3), custom_call_target="tpu_custom_call" | custom-call | flops 2147483648 | bytes 3145728 | tf_op jit(solution)/shard_map/pick_first/pallas_call | solution.py:80
  5.1 0.0 copy-done.3
  5.2 0.6 broadcast_in_dim.14
  5.8 15.2 %all-to-all-start = ((bf16[16,16,128]{2,1,0:T(8,128)(2,1)}), bf16[16,16,128]{2,1,0:T(8,128)(2,1)S(1)}, u32[]{:S(2)}, u32[]{:S(2)}) async-start(bf16[16,16,128]{2,1,0:T(8,128)(2,1)} %broadcast_in_dim.14), calls=%async_computation | async-start | bytes 131072 | tf_op jit(solution)/shard_map/all_to_all | solution.py:151
  21.0 11.8 %all-to-all-done = bf16[16,16,128]{2,1,0:T(8,128)(2,1)S(1)} async-done(((bf16[16,16,128]{2,1,0:T(8,128)(2,1)}), bf16[16,16,128]{2,1,0:T(8,128)(2,1)S(1)}, u32[]{:S(2)}, u32[]{:S(2)}) %all-to-all-start) | async-done | bytes 65568 | tf_op jit(solution)/shard_map/all_to_all | solution.py:151
  32.9 0.1 broadcast_in_dim.15
  33.0 0.0 copy-start
  33.0 0.0 copy-start.1
  33.0 0.0 copy-start.2
  33.0 19.9 %all_to_all.20 = bf16[16,16,2048]{2,1,0:T(8,128)(2,1)S(1)} all-to-all(bf16[16,16,2048]{2,1,0:T(8,128)(2,1)S(1)} %broadcast_in_dim.15), channel_id=1, replica_groups=mesh['half'=2,'x'=4,'y'=4,'z'=16] {'x','y'}, dimensions={0} | all-to-all | bytes 2097152 | tf_op jit(solution)/shard_map/all_to_all | solution.py:156
  52.9 0.0 copy-done
  52.9 0.0 copy-done.1
  52.9 0.0 copy-done.2
  52.9 3.3 %expect.1 = (bf16[16,16,2176]{2,1,0:T(8,128)(2,1)S(1)}, f32[1,256]{1,0:T(1,128)}) custom-call(bf16[256,2048]{1,0:T(8,128)(2,1)S(1)} %copy-done, bf16[256,2048]{1,0:T(8,128)(2,1)S(1)} %bitcast.9, bf16[256,1024]{1,0:T(8,128)(2,1)S(1)} %copy-done.2, f32[1,256]{1,0:T(1,128)S(1)} %bitcast.10), custom_call_target="tpu_custom_call" | custom-call | flops 1400000000 | bytes 4194304 | tf_op jit(solution)/shard_map/expect/pallas_call | solution.py:132
  56.2 16.5 %all_to_all.21 = bf16[16,16,2176]{2,1,0:T(8,128)(2,1)S(1)} all-to-all(bf16[16,16,2176]{2,1,0:T(8,128)(2,1)S(1)} %get-tuple-element.12), channel_id=1, replica_groups=mesh['half'=2,'x'=4,'y'=4,'z'=16] {'x','y'}, dimensions={0} | all-to-all | bytes 2228224 | tf_op jit(solution)/shard_map/all_to_all | solution.py:169
  72.7 0.2 reduce_sum.12
  72.9 16.6 %all_to_all.22.column_ref = bf16[16,17,128]{2,1,0:T(8,128)(2,1)S(1)} all-to-all(bf16[16,17,128]{2,1,0:T(8,128)(2,1)S(1)} %reshape.28), channel_id=1, replica_groups=mesh['half'=2,'x'=4,'y'=4,'z'=16] {'z'}, dimensions={0} | all-to-all | bytes 139264 | tf_op jit(solution)/shard_map/all_to_all | solution.py:171
  89.5 0.7 finish.1
  (4 shorter events, 0.1 us)
Async XLA Ops:
  0.6 4.5 %copy-start.3 = (bf16[1,2048]{1,0:T(2,128)(2,1)S(1)}, bf16[1,2048]{1,0:T(2,128)(2,1)}, u32[]{:S(2)}) copy-start(bf16[1,2048]{1,0:T(2,128)(2,1)} %param.7) | copy-start | bytes 12292
  5.8 27.0 %all-to-all-start = ((bf16[16,16,128]{2,1,0:T(8,128)(2,1)}), bf16[16,16,128]{2,1,0:T(8,128)(2,1)S(1)}, u32[]{:S(2)}, u32[]{:S(2)}) async-start(bf16[16,16,128]{2,1,0:T(8,128)(2,1)} %broadcast_in_dim.14), calls=%async_computation | async-start | bytes 131072 | tf_op jit(solution)/shard_map/all_to_all | solution.py:151
  33.0 19.9 %copy-start = (bf16[256,2048]{1,0:T(8,128)(2,1)S(1)}, bf16[256,2048]{1,0:T(8,128)(2,1)}, u32[]{:S(2)}) copy-start(bf16[256,2048]{1,0:T(8,128)(2,1)} %images_ref.1) | copy-start | bytes 3145732
  33.0 19.9 %copy-start.1 = (f32[256]{0:T(256)S(1)}, f32[256]{0:T(256)}, u32[]{:S(2)}) copy-start(f32[256]{0:T(256)} %param.9) | copy-start | bytes 3076
  33.0 19.9 %copy-start.2 = (bf16[256,1024]{1,0:T(8,128)(2,1)S(1)}, bf16[256,1024]{1,0:T(8,128)(2,1)}, u32[]{:S(2)}) copy-start(bf16[256,1024]{1,0:T(8,128)(2,1)} %pick_second.1.picked_ref) | copy-start | bytes 1572868

commit v6 on v5

--- a/solution.py
+++ b/solution.py
@@ -9,6 +9,7 @@
 PLANE = ("x", "y")
 SLABS, FREQ, ORI, SUB, ROWS = 256, 2048, 4096, 1024, 256
 WIDE = FREQ + 128
+PAIR = 1152
 BF16, F32 = jnp.bfloat16, jnp.float32
 NN = (((1,), (0,)), ((), ()))
 NT = (((1,), (1,)), ((), ()))
@@ -161,14 +162,16 @@
 
 def finish_kernel(column_ref, new_ref):
     total = jnp.sum(column_ref[...].astype(F32), axis=0)
-    weight = total[FREQ // 128 :, :1] + total[FREQ // 128 :, 1:2]
-    new_ref[...] = total[: FREQ // 128, :] / (weight + 1.0)
+    lanes = [total[r : r + 1, c : c + 128] for r in range(2) for c in range(0, PAIR, 128)]
+    weight = lanes[FREQ // 128][:, :1] + lanes[FREQ // 128][:, 1:2]
+    new_ref[...] = jnp.concatenate(lanes[: FREQ // 128], axis=0) / (weight + 1.0)
 
 
 def new_slab(partial):
     plane = lax.all_to_all(partial, PLANE, 0, 0, tiled=True)
     plane = jnp.sum(plane.astype(F32), axis=0).astype(BF16)
-    column = lax.all_to_all(plane.reshape(Z, WIDE // 128, 128), "z", 0, 0, tiled=True)
+    plane = jnp.pad(plane, ((0, 0), (0, 2 * PAIR - WIDE))).reshape(Z, 2, PAIR)
+    column = lax.all_to_all(plane, "z", 0, 0, tiled=True)
     return pl.pallas_call(
         finish_kernel,
         out_shape=jax.ShapeDtypeStruct((FREQ // 128, 128), F32),

time: 90.6 us -> 90.3 us (level)
  no operation moved by 1% of the time
where the time goes in v6:
time: 90.3 us; the launch traced here: 90 us
  blocking collectives  52.6 us (58%)
  starting transfers between devices  15.2 us (17%)
  waiting for transfers between devices  11.8 us (13%)
  Pallas kernels  8.6 us (10%)
    all_to_all x1, blocking collectives, gather_slabs(): lax.all_to_all(jnp.broadcast_to(column[None], (X * Y, Z, FREQ)), PLANE, 0...  19.9 us
    all_to_all x1, blocking collectives, new_slab(): plane = lax.all_to_all(partial, PLANE, 0, 0, tiled=True)  16.5 us
    all_to_all x1, blocking collectives, new_slab(): column = lax.all_to_all(plane, 'z', 0, 0, tiled=True)  16.2 us
    all_to_all x1, starting transfers between devices, gather_slabs(): lax.all_to_all(jnp.broadcast_to(volume.reshape(1, 16, 128), (Z, 16, 128))...  15.2 us
    all_to_all x1, waiting for transfers between devices, gather_slabs(): lax.all_to_all(jnp.broadcast_to(volume.reshape(1, 16, 128), (Z, 16, 128))...  11.8 us
    pallas_call x2, Pallas kernels, pick(): pl.pallas_call(kernel, out_shape=jax.ShapeDtypeStruct((SLABS, SUB), BF16)...  4.5 us
    pallas_call x1, Pallas kernels, expect(): pl.pallas_call(expect_kernel, out_shape=(jax.ShapeDtypeStruct((X * Y, Z,...  3.32 us
  transfers between devices with their start and end apart: 1, of which 1 were waited for; matrix products, arithmetic and copies ran while one was open for 0% of the time, Pallas kernels for 0%

profile of v6, /device:TPU:32, one launch (start us, length us, event | category | flops | bytes accessed | tf_op | source)
XLA Modules:
  0.0 90.0 jit_solution(7047816369877347591)
XLA Ops:
  0.6 0.0 copy-start.3
  0.6 4.5 %pick_first.1.held_ref = bf16[256,1024]{1,0:T(8,128)(2,1)} custom-call(s32[1,1024]{1,0:T(1,128)} %subset_hbm.3, bf16[4096,256]{1,0:T(8,128)(2,1)} %projection_hbm.3), custom_call_target="tpu_custom_call" | custom-call | flops 2147483648 | bytes 3145728 | tf_op jit(solution)/shard_map/pick_first/pallas_call | solution.py:81
  5.1 0.0 copy-done.3
  5.2 0.6 broadcast_in_dim.14
  5.8 15.2 %all-to-all-start = ((bf16[16,16,128]{2,1,0:T(8,128)(2,1)}), bf16[16,16,128]{2,1,0:T(8,128)(2,1)S(1)}, u32[]{:S(2)}, u32[]{:S(2)}) async-start(bf16[16,16,128]{2,1,0:T(8,128)(2,1)} %broadcast_in_dim.14), calls=%async_computation | async-start | bytes 131072 | tf_op jit(solution)/shard_map/all_to_all | solution.py:152
  21.0 11.8 %all-to-all-done = bf16[16,16,128]{2,1,0:T(8,128)(2,1)S(1)} async-done(((bf16[16,16,128]{2,1,0:T(8,128)(2,1)}), bf16[16,16,128]{2,1,0:T(8,128)(2,1)S(1)}, u32[]{:S(2)}, u32[]{:S(2)}) %all-to-all-start) | async-done | bytes 65568 | tf_op jit(solution)/shard_map/all_to_all | solution.py:152
  32.9 0.1 broadcast_in_dim.15
  33.0 0.0 copy-start
  33.0 0.0 copy-start.1
  33.0 0.0 copy-start.2
  33.0 19.9 %all_to_all.20 = bf16[16,16,2048]{2,1,0:T(8,128)(2,1)S(1)} all-to-all(bf16[16,16,2048]{2,1,0:T(8,128)(2,1)S(1)} %broadcast_in_dim.15), channel_id=1, replica_groups=mesh['half'=2,'x'=4,'y'=4,'z'=16] {'x','y'}, dimensions={0} | all-to-all | bytes 2097152 | tf_op jit(solution)/shard_map/all_to_all | solution.py:157
  52.9 0.0 copy-done
  52.9 0.0 copy-done.1
  52.9 0.0 copy-done.2
  52.9 3.3 %expect.1 = (bf16[16,16,2176]{2,1,0:T(8,128)(2,1)S(1)}, f32[1,256]{1,0:T(1,128)}) custom-call(bf16[256,2048]{1,0:T(8,128)(2,1)S(1)} %copy-done, bf16[256,2048]{1,0:T(8,128)(2,1)S(1)} %bitcast.9, bf16[256,1024]{1,0:T(8,128)(2,1)S(1)} %copy-done.2, f32[1,256]{1,0:T(1,128)S(1)} %bitcast.10), custom_call_target="tpu_custom_call" | custom-call | flops 1400000000 | bytes 4194304 | tf_op jit(solution)/shard_map/expect/pallas_call | solution.py:133
  56.2 16.5 %all_to_all.21 = bf16[16,16,2176]{2,1,0:T(8,128)(2,1)S(1)} all-to-all(bf16[16,16,2176]{2,1,0:T(8,128)(2,1)S(1)} %get-tuple-element.12), channel_id=1, replica_groups=mesh['half'=2,'x'=4,'y'=4,'z'=16] {'x','y'}, dimensions={0} | all-to-all | bytes 2228224 | tf_op jit(solution)/shard_map/all_to_all | solution.py:171
  72.7 0.2 reduce_sum.12
  72.9 16.2 %all_to_all.22.column_ref = bf16[16,2,1152]{2,1,0:T(2,128)(2,1)S(1)} all-to-all(bf16[16,2,1152]{2,1,0:T(2,128)(2,1)S(1)} %reshape.28), channel_id=1, replica_groups=mesh['half'=2,'x'=4,'y'=4,'z'=16] {'z'}, dimensions={0} | all-to-all | bytes 147456 | tf_op jit(solution)/shard_map/all_to_all | solution.py:174
  89.2 0.8 finish.1
  (5 shorter events, 0.1 us)
Async XLA Ops:
  0.6 4.5 %copy-start.3 = (bf16[1,2048]{1,0:T(2,128)(2,1)S(1)}, bf16[1,2048]{1,0:T(2,128)(2,1)}, u32[]{:S(2)}) copy-start(bf16[1,2048]{1,0:T(2,128)(2,1)} %param.7) | copy-start | bytes 12292
  5.8 27.0 %all-to-all-start = ((bf16[16,16,128]{2,1,0:T(8,128)(2,1)}), bf16[16,16,128]{2,1,0:T(8,128)(2,1)S(1)}, u32[]{:S(2)}, u32[]{:S(2)}) async-start(bf16[16,16,128]{2,1,0:T(8,128)(2,1)} %broadcast_in_dim.14), calls=%async_computation | async-start | bytes 131072 | tf_op jit(solution)/shard_map/all_to_all | solution.py:152
  33.0 19.9 %copy-start = (bf16[256,2048]{1,0:T(8,128)(2,1)S(1)}, bf16[256,2048]{1,0:T(8,128)(2,1)}, u32[]{:S(2)}) copy-start(bf16[256,2048]{1,0:T(8,128)(2,1)} %images_ref.1) | copy-start | bytes 3145732
  33.0 19.9 %copy-start.1 = (f32[256]{0:T(256)S(1)}, f32[256]{0:T(256)}, u32[]{:S(2)}) copy-start(f32[256]{0:T(256)} %param.9) | copy-start | bytes 3076
  33.0 19.9 %copy-start.2 = (bf16[256,1024]{1,0:T(8,128)(2,1)S(1)}, bf16[256,1024]{1,0:T(8,128)(2,1)}, u32[]{:S(2)}) copy-start(bf16[256,1024]{1,0:T(8,128)(2,1)} %pick_second.1.picked_ref) | copy-start | bytes 1572868

commit v7 on v6

--- a/solution.py
+++ b/solution.py
@@ -28,7 +28,7 @@
     return found
 
 
-BLOCKS = 2
+BLOCKS = 4
 BLOCK = ORI // BLOCKS
 
 
@@ -104,9 +104,9 @@
     picked = picked_ref[...]
     gram = mm(volume, volume, NT)
     cross = mm(images, volume, NT)
-    many = mm(jnp.concatenate(parts(gram, 3) + parts(cross, 3), axis=0), picked, NN)
+    many = mm(jnp.concatenate(parts(gram, 3) + parts(cross, 2), axis=0), picked, NN)
     wide = sum(many[k * SLABS : (k + 1) * SLABS] for k in range(3))
-    correlate = sum(many[k * ROWS : (k + 1) * ROWS] for k in range(3, 6))
+    correlate = sum(many[k * ROWS : (k + 1) * ROWS] for k in range(3, 5))
     pfloat = picked.astype(F32)
     energy = jnp.sum(wide * pfloat, axis=0, keepdims=True)
     precision = jnp.transpose(jnp.broadcast_to(precision_ref[...], (128, ROWS)))[:, :1]
@@ -146,11 +146,40 @@
     )(images, volume, picked, precision)
 
 
+def spread_kernel(row_hbm, spread_hbm, row_ref, spread_ref, sem):
+    come = pltpu.make_async_copy(row_hbm, row_ref, sem)
+    come.start()
+    come.wait()
+    row = jnp.concatenate([row_ref[:, c * 128 : (c + 1) * 128] for c in range(16)], axis=0)
+    for z in range(Z):
+        spread_ref[z] = row
+    go = pltpu.make_async_copy(spread_ref, spread_hbm, sem)
+    go.start()
+    go.wait()
+
+
+def spread(volume):
+    return pl.pallas_call(
+        spread_kernel,
+        out_shape=jax.ShapeDtypeStruct((Z, 16, 128), BF16),
+        in_specs=[pl.BlockSpec(memory_space=pltpu.HBM)],
+        out_specs=pl.BlockSpec(memory_space=pltpu.HBM),
+        scratch_shapes=[
+            pltpu.VMEM((1, FREQ), BF16),
+            pltpu.VMEM((Z, 16, 128), BF16),
+            pltpu.SemaphoreType.DMA,
+        ],
+        compiler_params=pltpu.CompilerParams(vmem_limit_bytes=60 << 20),
+        cost_estimate=pl.CostEstimate(flops=1000, bytes_accessed=1 << 16, transcendentals=0),
+        name="spread",
+    )(volume)
+
+
 def gather_slabs(volume, subset, projection):
     picked = pick(pick_first_kernel, "pick_first", subset, projection)
     volume, picked = lax.optimization_barrier((volume, picked))
     column = lax.all_to_all(
-        jnp.broadcast_to(volume.reshape(1, 16, 128), (Z, 16, 128)), "z", 0, 0, tiled=True
+        spread(volume), "z", 0, 0, tiled=True
     )
     picked = pick(pick_second_kernel, "pick_second", subset, projection, picked)
     column, picked = lax.optimization_barrier((column.reshape(Z, FREQ), picked))

time: 90.3 us -> 90.3 us (level)
  Pallas kernels: 8.6 us -> 9.84 us
    pallas_call x0 -> x1, Pallas kernels: none -> 1.35 us  [spread(): pl.pallas_call(spread_kernel, out_shape=jax.ShapeDtypeStruct((Z, 16, 128)...]
where the time goes in v7:
time: 90.3 us; the launch traced here: 89.9 us
  blocking collectives  52 us (58%)
  starting transfers between devices  15.2 us (17%)
  waiting for transfers between devices  11.8 us (13%)
  Pallas kernels  9.84 us (11%)
    all_to_all x1, blocking collectives, gather_slabs(): lax.all_to_all(jnp.broadcast_to(column[None], (X * Y, Z, FREQ)), PLANE, 0...  19.9 us
    all_to_all x1, blocking collectives, new_slab(): plane = lax.all_to_all(partial, PLANE, 0, 0, tiled=True)  16.5 us
    all_to_all x1, blocking collectives, new_slab(): column = lax.all_to_all(plane, 'z', 0, 0, tiled=True)  15.6 us
    all_to_all x1, starting transfers between devices, gather_slabs(): column = lax.all_to_all(spread(volume), 'z', 0, 0, tiled=True)  15.2 us
    all_to_all x1, waiting for transfers between devices, gather_slabs(): column = lax.all_to_all(spread(volume), 'z', 0, 0, tiled=True)  11.8 us
    pallas_call x2, Pallas kernels, pick(): pl.pallas_call(kernel, out_shape=jax.ShapeDtypeStruct((SLABS, SUB), BF16)...  4.52 us
    pallas_call x1, Pallas kernels, expect(): pl.pallas_call(expect_kernel, out_shape=(jax.ShapeDtypeStruct((X * Y, Z,...  3.2 us
  transfers between devices with their start and end apart: 1, of which 1 were waited for; matrix products, arithmetic and copies ran while one was open for 0% of the time, Pallas kernels for 0%

profile of v7, /device:TPU:32, one launch (start us, length us, event | category | flops | bytes accessed | tf_op | source)
XLA Modules:
  0.0 89.9 jit_solution(14956716139296244815)
XLA Ops:
  0.6 4.5 %pick_first.1.held_ref = bf16[256,1024]{1,0:T(8,128)(2,1)} custom-call(s32[1,1024]{1,0:T(1,128)} %subset_hbm.3, bf16[4096,256]{1,0:T(8,128)(2,1)} %projection_hbm.3), custom_call_target="tpu_custom_call" | custom-call | flops 2147483648 | bytes 3145728 | tf_op jit(solution)/shard_map/pick_first/pallas_call | solution.py:81
  5.1 1.4 %spread.1 = bf16[16,16,128]{2,1,0:T(8,128)(2,1)} custom-call(bf16[1,2048]{1,0:T(2,128)(2,1)} %row_hbm), custom_call_target="tpu_custom_call" | custom-call | flops 1000 | bytes 65536 | tf_op jit(solution)/shard_map/spread/pallas_call | solution.py:162
  6.5 15.2 %all-to-all-start = ((bf16[16,16,128]{2,1,0:T(8,128)(2,1)}), bf16[16,16,128]{2,1,0:T(8,128)(2,1)S(1)}, u32[]{:S(2)}, u32[]{:S(2)}) async-start(bf16[16,16,128]{2,1,0:T(8,128)(2,1)} %spread.1), calls=%async_computation | async-start | bytes 131072 | tf_op jit(solution)/shard_map/all_to_all | solution.py:181
  21.7 11.8 %all-to-all-done = bf16[16,16,128]{2,1,0:T(8,128)(2,1)S(1)} async-done(((bf16[16,16,128]{2,1,0:T(8,128)(2,1)}), bf16[16,16,128]{2,1,0:T(8,128)(2,1)S(1)}, u32[]{:S(2)}, u32[]{:S(2)}) %all-to-all-start) | async-done | bytes 65568 | tf_op jit(solution)/shard_map/all_to_all | solution.py:181
  33.5 0.1 broadcast_in_dim.2
  33.7 0.0 copy-start
  33.7 0.0 copy-start.1
  33.7 0.0 copy-start.2
  33.7 19.9 %all_to_all.20 = bf16[16,16,2048]{2,1,0:T(8,128)(2,1)S(1)} all-to-all(bf16[16,16,2048]{2,1,0:T(8,128)(2,1)S(1)} %broadcast_in_dim.2), channel_id=1, replica_groups=mesh['half'=2,'x'=4,'y'=4,'z'=16] {'x','y'}, dimensions={0} | all-to-all | bytes 2097152 | tf_op jit(solution)/shard_map/all_to_all | solution.py:186
  53.6 0.0 copy-done
  53.6 0.0 copy-done.1
  53.6 0.0 copy-done.2
  53.6 3.2 %expect.1 = (bf16[16,16,2176]{2,1,0:T(8,128)(2,1)S(1)}, f32[1,256]{1,0:T(1,128)}) custom-call(bf16[256,2048]{1,0:T(8,128)(2,1)S(1)} %copy-done, bf16[256,2048]{1,0:T(8,128)(2,1)S(1)} %bitcast.8, bf16[256,1024]{1,0:T(8,128)(2,1)S(1)} %copy-done.2, f32[1,256]{1,0:T(1,128)S(1)} %bitcast.9), custom_call_target="tpu_custom_call" | custom-call | flops 1400000000 | bytes 4194304 | tf_op jit(solution)/shard_map/expect/pallas_call | solution.py:133
  56.8 16.5 %all_to_all.21 = bf16[16,16,2176]{2,1,0:T(8,128)(2,1)S(1)} all-to-all(bf16[16,16,2176]{2,1,0:T(8,128)(2,1)S(1)} %get-tuple-element.12), channel_id=1, replica_groups=mesh['half'=2,'x'=4,'y'=4,'z'=16] {'x','y'}, dimensions={0} | all-to-all | bytes 2228224 | tf_op jit(solution)/shard_map/all_to_all | solution.py:200
  73.3 0.2 reduce_sum.12
  73.5 15.6 %all_to_all.22.column_ref = bf16[16,2,1152]{2,1,0:T(2,128)(2,1)S(1)} all-to-all(bf16[16,2,1152]{2,1,0:T(2,128)(2,1)S(1)} %reshape.26), channel_id=1, replica_groups=mesh['half'=2,'x'=4,'y'=4,'z'=16] {'z'}, dimensions={0} | all-to-all | bytes 147456 | tf_op jit(solution)/shard_map/all_to_all | solution.py:203
  89.1 0.8 finish.1
  (4 shorter events, 0.1 us)
Async XLA Ops:
  6.5 27.0 %all-to-all-start = ((bf16[16,16,128]{2,1,0:T(8,128)(2,1)}), bf16[16,16,128]{2,1,0:T(8,128)(2,1)S(1)}, u32[]{:S(2)}, u32[]{:S(2)}) async-start(bf16[16,16,128]{2,1,0:T(8,128)(2,1)} %spread.1), calls=%async_computation | async-start | bytes 131072 | tf_op jit(solution)/shard_map/all_to_all | solution.py:181
  33.7 19.9 %copy-start = (bf16[256,2048]{1,0:T(8,128)(2,1)S(1)}, bf16[256,2048]{1,0:T(8,128)(2,1)}, u32[]{:S(2)}) copy-start(bf16[256,2048]{1,0:T(8,128)(2,1)} %images_ref.1) | copy-start | bytes 3145732
  33.7 19.9 %copy-start.1 = (f32[256]{0:T(256)S(1)}, f32[256]{0:T(256)}, u32[]{:S(2)}) copy-start(f32[256]{0:T(256)} %param.9) | copy-start | bytes 3076
  33.7 19.9 %copy-start.2 = (bf16[256,1024]{1,0:T(8,128)(2,1)S(1)}, bf16[256,1024]{1,0:T(8,128)(2,1)}, u32[]{:S(2)}) copy-start(bf16[256,1024]{1,0:T(8,128)(2,1)} %pick_second.1.picked_ref) | copy-start | bytes 1572868

commit v8 on v7

--- a/solution.py
+++ b/solution.py
@@ -110,16 +110,20 @@
     pfloat = picked.astype(F32)
     energy = jnp.sum(wide * pfloat, axis=0, keepdims=True)
     precision = jnp.transpose(jnp.broadcast_to(precision_ref[...], (128, ROWS)))[:, :1]
-    scores = precision * (correlate - 0.5 * energy)
-    highest = jnp.max(scores, axis=1, keepdims=True)
-    expo = jnp.exp(scores - highest)
-    summed = jnp.sum(expo, axis=1, keepdims=True)
-    evidence = highest + jnp.log(summed)
+    occupancy, mixed, seen = 0.0, [], []
+    for r in range(0, ROWS, 128):
+        scores = precision[r : r + 128] * (correlate[r : r + 128] - 0.5 * energy)
+        highest = jnp.max(scores, axis=1, keepdims=True)
+        expo = jnp.exp(scores - highest)
+        summed = jnp.sum(expo, axis=1, keepdims=True)
+        seen.append(highest + jnp.log(summed))
+        weights = expo * (1.0 / summed)
+        occupancy += jnp.sum(weights, axis=0, keepdims=True)
+        mixed.append(mm(picked, weights.astype(BF16), NT).astype(BF16))
+    evidence = jnp.concatenate(seen, axis=0)
     evidence_ref[...] = jnp.transpose(jnp.broadcast_to(evidence, (ROWS, 128)))[:1, :]
-    weights = expo * (1.0 / summed)
-    occupancy = jnp.sum(weights, axis=0, keepdims=True)
     slab_weight = jnp.sum(occupancy * (pfloat * pfloat), axis=1, keepdims=True)
-    mixed = mm(picked, weights.astype(BF16), NT).astype(BF16)
+    mixed = jnp.concatenate(mixed, axis=1)
     for c in range(0, FREQ, 512):
         numer = mm(mixed, images_ref[:, c : c + 512], NN)
         partial_ref[:, :, c : c + 512] = numer.astype(BF16).reshape(X * Y, Z, 512)

time: 90.3 us -> 90.1 us (level)
  no operation moved by 1% of the time
where the time goes in v8:
time: 90.1 us; the launch traced here: 89.8 us
  blocking collectives  52 us (58%)
  starting transfers between devices  15.2 us (17%)
  waiting for transfers between devices  11.8 us (13%)
  Pallas kernels  9.7 us (11%)
    all_to_all x1, blocking collectives, gather_slabs(): lax.all_to_all(jnp.broadcast_to(column[None], (X * Y, Z, FREQ)), PLANE, 0...  19.9 us
    all_to_all x1, blocking collectives, new_slab(): plane = lax.all_to_all(partial, PLANE, 0, 0, tiled=True)  16.5 us
    all_to_all x1, blocking collectives, new_slab(): column = lax.all_to_all(plane, 'z', 0, 0, tiled=True)  15.6 us
    all_to_all x1, starting transfers between devices, gather_slabs(): column = lax.all_to_all(spread(volume), 'z', 0, 0, tiled=True)  15.2 us
    all_to_all x1, waiting for transfers between devices, gather_slabs(): column = lax.all_to_all(spread(volume), 'z', 0, 0, tiled=True)  11.8 us
    pallas_call x2, Pallas kernels, pick(): pl.pallas_call(kernel, out_shape=jax.ShapeDtypeStruct((SLABS, SUB), BF16)...  4.52 us
    pallas_call x1, Pallas kernels, expect(): pl.pallas_call(expect_kernel, out_shape=(jax.ShapeDtypeStruct((X * Y, Z,...  3.05 us
  transfers between devices with their start and end apart: 1, of which 1 were waited for; matrix products, arithmetic and copies ran while one was open for 0% of the time, Pallas kernels for 0%

profile of v8, /device:TPU:32, one launch (start us, length us, event | category | flops | bytes accessed | tf_op | source)
XLA Modules:
  0.0 89.8 jit_solution(1015671847266140937)
XLA Ops:
  0.6 4.5 %pick_first.1.held_ref = bf16[256,1024]{1,0:T(8,128)(2,1)} custom-call(s32[1,1024]{1,0:T(1,128)} %subset_hbm.3, bf16[4096,256]{1,0:T(8,128)(2,1)} %projection_hbm.3), custom_call_target="tpu_custom_call" | custom-call | flops 2147483648 | bytes 3145728 | tf_op jit(solution)/shard_map/pick_first/pallas_call | solution.py:81
  5.1 1.4 %spread.1 = bf16[16,16,128]{2,1,0:T(8,128)(2,1)} custom-call(bf16[1,2048]{1,0:T(2,128)(2,1)} %row_hbm), custom_call_target="tpu_custom_call" | custom-call | flops 1000 | bytes 65536 | tf_op jit(solution)/shard_map/spread/pallas_call | solution.py:166
  6.5 15.2 %all-to-all-start = ((bf16[16,16,128]{2,1,0:T(8,128)(2,1)}), bf16[16,16,128]{2,1,0:T(8,128)(2,1)S(1)}, u32[]{:S(2)}, u32[]{:S(2)}) async-start(bf16[16,16,128]{2,1,0:T(8,128)(2,1)} %spread.1), calls=%async_computation | async-start | bytes 131072 | tf_op jit(solution)/shard_map/all_to_all | solution.py:185
  21.7 11.8 %all-to-all-done = bf16[16,16,128]{2,1,0:T(8,128)(2,1)S(1)} async-done(((bf16[16,16,128]{2,1,0:T(8,128)(2,1)}), bf16[16,16,128]{2,1,0:T(8,128)(2,1)S(1)}, u32[]{:S(2)}, u32[]{:S(2)}) %all-to-all-start) | async-done | bytes 65568 | tf_op jit(solution)/shard_map/all_to_all | solution.py:185
  33.5 0.1 broadcast_in_dim.2
  33.7 0.0 copy-start
  33.7 0.0 copy-start.1
  33.7 0.0 copy-start.2
  33.7 19.9 %all_to_all.20 = bf16[16,16,2048]{2,1,0:T(8,128)(2,1)S(1)} all-to-all(bf16[16,16,2048]{2,1,0:T(8,128)(2,1)S(1)} %broadcast_in_dim.2), channel_id=1, replica_groups=mesh['half'=2,'x'=4,'y'=4,'z'=16] {'x','y'}, dimensions={0} | all-to-all | bytes 2097152 | tf_op jit(solution)/shard_map/all_to_all | solution.py:190
  53.6 0.0 copy-done
  53.6 0.0 copy-done.1
  53.6 0.0 copy-done.2
  53.6 3.1 %expect.1 = (bf16[16,16,2176]{2,1,0:T(8,128)(2,1)S(1)}, f32[1,256]{1,0:T(1,128)}) custom-call(bf16[256,2048]{1,0:T(8,128)(2,1)S(1)} %copy-done, bf16[256,2048]{1,0:T(8,128)(2,1)S(1)} %bitcast.8, bf16[256,1024]{1,0:T(8,128)(2,1)S(1)} %copy-done.2, f32[1,256]{1,0:T(1,128)S(1)} %bitcast.9), custom_call_target="tpu_custom_call" | custom-call | flops 1400000000 | bytes 4194304 | tf_op jit(solution)/shard_map/expect/pallas_call | solution.py:137
  56.6 16.5 %all_to_all.21 = bf16[16,16,2176]{2,1,0:T(8,128)(2,1)S(1)} all-to-all(bf16[16,16,2176]{2,1,0:T(8,128)(2,1)S(1)} %get-tuple-element.12), channel_id=1, replica_groups=mesh['half'=2,'x'=4,'y'=4,'z'=16] {'x','y'}, dimensions={0} | all-to-all | bytes 2228224 | tf_op jit(solution)/shard_map/all_to_all | solution.py:204
  73.1 0.2 reduce_sum.12
  73.3 15.6 %all_to_all.22.column_ref = bf16[16,2,1152]{2,1,0:T(2,128)(2,1)S(1)} all-to-all(bf16[16,2,1152]{2,1,0:T(2,128)(2,1)S(1)} %reshape.26), channel_id=1, replica_groups=mesh['half'=2,'x'=4,'y'=4,'z'=16] {'z'}, dimensions={0} | all-to-all | bytes 147456 | tf_op jit(solution)/shard_map/all_to_all | solution.py:207
  89.0 0.8 finish.1
  (4 shorter events, 0.1 us)
Async XLA Ops:
  6.5 27.0 %all-to-all-start = ((bf16[16,16,128]{2,1,0:T(8,128)(2,1)}), bf16[16,16,128]{2,1,0:T(8,128)(2,1)S(1)}, u32[]{:S(2)}, u32[]{:S(2)}) async-start(bf16[16,16,128]{2,1,0:T(8,128)(2,1)} %spread.1), calls=%async_computation | async-start | bytes 131072 | tf_op jit(solution)/shard_map/all_to_all | solution.py:185
  33.7 19.9 %copy-start = (bf16[256,2048]{1,0:T(8,128)(2,1)S(1)}, bf16[256,2048]{1,0:T(8,128)(2,1)}, u32[]{:S(2)}) copy-start(bf16[256,2048]{1,0:T(8,128)(2,1)} %images_ref.1) | copy-start | bytes 3145732
  33.7 19.9 %copy-start.1 = (f32[256]{0:T(256)S(1)}, f32[256]{0:T(256)}, u32[]{:S(2)}) copy-start(f32[256]{0:T(256)} %param.9) | copy-start | bytes 3076
  33.7 19.9 %copy-start.2 = (bf16[256,1024]{1,0:T(8,128)(2,1)S(1)}, bf16[256,1024]{1,0:T(8,128)(2,1)}, u32[]{:S(2)}) copy-start(bf16[256,1024]{1,0:T(8,128)(2,1)} %pick_second.1.picked_ref) | copy-start | bytes 1572868

commit v9 on v6

--- a/solution.py
+++ b/solution.py
@@ -65,38 +65,75 @@
     out.wait()
 
 
-def pick_first_kernel(subset_hbm, projection_hbm, *refs):
+def pick_first_kernel(
+    subset_hbm, projection_hbm, row_hbm, picked_hbm, spread_hbm, row_ref, spread_ref, row_sem, *scratch
+):
+    come = pltpu.make_async_copy(row_hbm, row_ref, row_sem)
+    go = pltpu.make_async_copy(spread_ref, spread_hbm, row_sem)
+    come.start()
+    come.wait()
+    row = jnp.concatenate([row_ref[:, c * 128 : (c + 1) * 128] for c in range(16)], axis=0)
+    for z in range(Z):
+        spread_ref[z] = row
+    go.start()
+
     @pl.when(lax.axis_index("half") == 0)
     def _():
-        pick_rows(subset_hbm, projection_hbm, *refs)
-
-
-def pick_second_kernel(subset_hbm, projection_hbm, held_ref, *refs):
+        pick_rows(subset_hbm, projection_hbm, picked_hbm, *scratch)
+
+    go.wait()
+
+
+def pick_second_kernel(subset_hbm, projection_hbm, held_hbm, picked_hbm, *scratch):
     @pl.when(lax.axis_index("half") == 1)
     def _():
-        pick_rows(subset_hbm, projection_hbm, *refs)
-
-
-def pick(kernel, name, subset, projection, *held):
-    return pl.pallas_call(
-        kernel,
-        out_shape=jax.ShapeDtypeStruct((SLABS, SUB), BF16),
-        in_specs=[pl.BlockSpec(memory_space=pltpu.HBM)] * (2 + len(held)),
+        pick_rows(subset_hbm, projection_hbm, picked_hbm, *scratch)
+
+
+PICKED = jax.ShapeDtypeStruct((SLABS, SUB), BF16)
+SCRATCH = [
+    pltpu.VMEM((1, SUB), jnp.int32),
+    pltpu.VMEM((ORI, SLABS), BF16),
+    pltpu.VMEM((SLABS, SUB), F32),
+    pltpu.VMEM((SLABS, SUB), BF16),
+    pltpu.SemaphoreType.DMA((BLOCKS + 1,)),
+]
+PICK_PARAMS = dict(
+    compiler_params=pltpu.CompilerParams(vmem_limit_bytes=60 << 20),
+    cost_estimate=pl.CostEstimate(
+        flops=2 * SLABS * ORI * SUB, bytes_accessed=3 << 20, transcendentals=0
+    ),
+)
+
+
+def pick_first(subset, projection, row):
+    return pl.pallas_call(
+        pick_first_kernel,
+        out_shape=(PICKED, jax.ShapeDtypeStruct((Z, 16, 128), BF16)),
+        in_specs=[pl.BlockSpec(memory_space=pltpu.HBM)] * 3,
+        out_specs=[pl.BlockSpec(memory_space=pltpu.HBM)] * 2,
+        scratch_shapes=[
+            pltpu.VMEM((1, FREQ), BF16),
+            pltpu.VMEM((Z, 16, 128), BF16),
+            pltpu.SemaphoreType.DMA,
+        ]
+        + SCRATCH,
+        name="pick_first",
+        **PICK_PARAMS,
+    )(subset, projection, row)
+
+
+def pick_second(subset, projection, held):
+    return pl.pallas_call(
+        pick_second_kernel,
+        out_shape=PICKED,
+        in_specs=[pl.BlockSpec(memory_space=pltpu.HBM)] * 3,
         out_specs=pl.BlockSpec(memory_space=pltpu.HBM),
-        input_output_aliases={2: 0} if held else {},
-        scratch_shapes=[
-            pltpu.VMEM((1, SUB), jnp.int32),
-            pltpu.VMEM((ORI, SLABS), BF16),
-            pltpu.VMEM((SLABS, SUB), F32),
-            pltpu.VMEM((SLABS, SUB), BF16),
-            pltpu.SemaphoreType.DMA((BLOCKS + 1,)),
-        ],
-        compiler_params=pltpu.CompilerParams(vmem_limit_bytes=60 << 20),
-        cost_estimate=pl.CostEstimate(
-            flops=2 * SLABS * ORI * SUB, bytes_accessed=3 << 20, transcendentals=0
-        ),
-        name=name,
-    )(subset, projection, *held)
+        input_output_aliases={2: 0},
+        scratch_shapes=SCRATCH,
+        name="pick_second",
+        **PICK_PARAMS,
+    )(subset, projection, held)
 
 
 def expect_kernel(images_ref, volume_ref, picked_ref, precision_ref, partial_ref, evidence_ref):
@@ -104,22 +141,26 @@
     picked = picked_ref[...]
     gram = mm(volume, volume, NT)
     cross = mm(images, volume, NT)
-    many = mm(jnp.concatenate(parts(gram, 3) + parts(cross, 3), axis=0), picked, NN)
+    many = mm(jnp.concatenate(parts(gram, 3) + parts(cross, 2), axis=0), picked, NN)
     wide = sum(many[k * SLABS : (k + 1) * SLABS] for k in range(3))
-    correlate = sum(many[k * ROWS : (k + 1) * ROWS] for k in range(3, 6))
+    correlate = sum(many[k * ROWS : (k + 1) * ROWS] for k in range(3, 5))
     pfloat = picked.astype(F32)
     energy = jnp.sum(wide * pfloat, axis=0, keepdims=True)
     precision = jnp.transpose(jnp.broadcast_to(precision_ref[...], (128, ROWS)))[:, :1]
-    scores = precision * (correlate - 0.5 * energy)
-    highest = jnp.max(scores, axis=1, keepdims=True)
-    expo = jnp.exp(scores - highest)
-    summed = jnp.sum(expo, axis=1, keepdims=True)
-    evidence = highest + jnp.log(summed)
+    occupancy, mixed, seen = 0.0, [], []
+    for r in range(0, ROWS, 128):
+        scores = precision[r : r + 128] * (correlate[r : r + 128] - 0.5 * energy)
+        highest = jnp.max(scores, axis=1, keepdims=True)
+        expo = jnp.exp(scores - highest)
+        summed = jnp.sum(expo, axis=1, keepdims=True)
+        seen.append(highest + jnp.log(summed))
+        weights = expo * (1.0 / summed)
+        occupancy += jnp.sum(weights, axis=0, keepdims=True)
+        mixed.append(mm(picked, weights.astype(BF16), NT).astype(BF16))
+    evidence = jnp.concatenate(seen, axis=0)
     evidence_ref[...] = jnp.transpose(jnp.broadcast_to(evidence, (ROWS, 128)))[:1, :]
-    weights = expo * (1.0 / summed)
-    occupancy = jnp.sum(weights, axis=0, keepdims=True)
     slab_weight = jnp.sum(occupancy * (pfloat * pfloat), axis=1, keepdims=True)
-    mixed = mm(picked, weights.astype(BF16), NT).astype(BF16)
+    mixed = jnp.concatenate(mixed, axis=1)
     for c in range(0, FREQ, 512):
         numer = mm(mixed, images_ref[:, c : c + 512], NN)
         partial_ref[:, :, c : c + 512] = numer.astype(BF16).reshape(X * Y, Z, 512)
@@ -147,12 +188,9 @@
 
 
 def gather_slabs(volume, subset, projection):
-    picked = pick(pick_first_kernel, "pick_first", subset, projection)
-    volume, picked = lax.optimization_barrier((volume, picked))
-    column = lax.all_to_all(
-        jnp.broadcast_to(volume.reshape(1, 16, 128), (Z, 16, 128)), "z", 0, 0, tiled=True
-    )
-    picked = pick(pick_second_kernel, "pick_second", subset, projection, picked)
+    picked, rows = pick_first(subset, projection, volume)
+    column = lax.all_to_all(rows, "z", 0, 0, tiled=True)
+    picked = pick_second(subset, projection, picked)
     column, picked = lax.optimization_barrier((column.reshape(Z, FREQ), picked))
     whole = lax.all_to_all(
         jnp.broadcast_to(column[None], (X * Y, Z, FREQ)), PLANE, 0, 0, tiled=True

time: 90.3 us -> 90.1 us (level)
  no operation moved by 1% of the time
where the time goes in v9:
time: 90.1 us; the launch traced here: 89.7 us
  blocking collectives  52.6 us (58%)
  starting transfers between devices  15.2 us (17%)
  waiting for transfers between devices  11.8 us (13%)
  Pallas kernels  9.1 us (10%)
    all_to_all x1, blocking collectives, gather_slabs(): lax.all_to_all(jnp.broadcast_to(column[None], (X * Y, Z, FREQ)), PLANE, 0...  19.9 us
    all_to_all x1, blocking collectives, new_slab(): plane = lax.all_to_all(partial, PLANE, 0, 0, tiled=True)  16.5 us
    all_to_all x1, blocking collectives, new_slab(): column = lax.all_to_all(plane, 'z', 0, 0, tiled=True)  16.2 us
    all_to_all x1, starting transfers between devices, gather_slabs(): column = lax.all_to_all(rows, 'z', 0, 0, tiled=True)  15.2 us
    all_to_all x1, waiting for transfers between devices, gather_slabs(): column = lax.all_to_all(rows, 'z', 0, 0, tiled=True)  11.8 us
    pallas_call x1, Pallas kernels, pick_first(): pl.pallas_call(pick_first_kernel, out_shape=(PICKED, jax.ShapeDtypeStruct...  5.24 us
    pallas_call x1, Pallas kernels, expect(): pl.pallas_call(expect_kernel, out_shape=(jax.ShapeDtypeStruct((X * Y, Z,...  3.05 us
  transfers between devices with their start and end apart: 1, of which 1 were waited for; matrix products, arithmetic and copies ran while one was open for 0% of the time, Pallas kernels for 0%

profile of v9, /device:TPU:32, one launch (start us, length us, event | category | flops | bytes accessed | tf_op | source)
XLA Modules:
  0.0 89.7 jit_solution(13358360638117090763)
XLA Ops:
  0.6 5.2 %pick_first.1 = (bf16[256,1024]{1,0:T(8,128)(2,1)}, bf16[16,16,128]{2,1,0:T(8,128)(2,1)}) custom-call(s32[1,1024]{1,0:T(1,128)} %subset_hbm.3, bf16[4096,256]{1,0:T(8,128)(2,1)} %projection_hbm.3, bf16[1,2048]{1,0:T(2,128)(2,1)} %row_hbm.1), custom_call_target="tpu_custom_call" | custom-call | flops 2147483648 | bytes 3145728 | tf_op jit(solution)/shard_map/pick_first/pallas_call | solution.py:110
  5.9 15.2 %all-to-all-start = ((bf16[16,16,128]{2,1,0:T(8,128)(2,1)}), bf16[16,16,128]{2,1,0:T(8,128)(2,1)S(1)}, u32[]{:S(2)}, u32[]{:S(2)}) async-start(bf16[16,16,128]{2,1,0:T(8,128)(2,1)} %get-tuple-element.8), calls=%async_computation | async-start | bytes 131072 | tf_op jit(solution)/shard_map/all_to_all | solution.py:192
  21.1 11.8 %all-to-all-done = bf16[16,16,128]{2,1,0:T(8,128)(2,1)S(1)} async-done(((bf16[16,16,128]{2,1,0:T(8,128)(2,1)}), bf16[16,16,128]{2,1,0:T(8,128)(2,1)S(1)}, u32[]{:S(2)}, u32[]{:S(2)}) %all-to-all-start) | async-done | bytes 65568 | tf_op jit(solution)/shard_map/all_to_all | solution.py:192
  33.0 0.1 broadcast_in_dim.2
  33.1 0.0 copy-start
  33.1 0.0 copy-start.1
  33.1 0.0 copy-start.2
  33.1 19.9 %all_to_all.20 = bf16[16,16,2048]{2,1,0:T(8,128)(2,1)S(1)} all-to-all(bf16[16,16,2048]{2,1,0:T(8,128)(2,1)S(1)} %broadcast_in_dim.2), channel_id=1, replica_groups=mesh['half'=2,'x'=4,'y'=4,'z'=16] {'x','y'}, dimensions={0} | all-to-all | bytes 2097152 | tf_op jit(solution)/shard_map/all_to_all | solution.py:195
  53.0 0.0 copy-done
  53.0 0.0 copy-done.1
  53.0 0.0 copy-done.2
  53.0 3.0 %expect.1 = (bf16[16,16,2176]{2,1,0:T(8,128)(2,1)S(1)}, f32[1,256]{1,0:T(1,128)}) custom-call(bf16[256,2048]{1,0:T(8,128)(2,1)S(1)} %copy-done, bf16[256,2048]{1,0:T(8,128)(2,1)S(1)} %bitcast.8, bf16[256,1024]{1,0:T(8,128)(2,1)S(1)} %copy-done.2, f32[1,256]{1,0:T(1,128)S(1)} %bitcast.9), custom_call_target="tpu_custom_call" | custom-call | flops 1400000000 | bytes 4194304 | tf_op jit(solution)/shard_map/expect/pallas_call | solution.py:174
  56.0 16.5 %all_to_all.21 = bf16[16,16,2176]{2,1,0:T(8,128)(2,1)S(1)} all-to-all(bf16[16,16,2176]{2,1,0:T(8,128)(2,1)S(1)} %get-tuple-element.12), channel_id=1, replica_groups=mesh['half'=2,'x'=4,'y'=4,'z'=16] {'x','y'}, dimensions={0} | all-to-all | bytes 2228224 | tf_op jit(solution)/shard_map/all_to_all | solution.py:209
  72.6 0.2 reduce_sum.12
  72.8 16.2 %all_to_all.22.column_ref = bf16[16,2,1152]{2,1,0:T(2,128)(2,1)S(1)} all-to-all(bf16[16,2,1152]{2,1,0:T(2,128)(2,1)S(1)} %reshape.26), channel_id=1, replica_groups=mesh['half'=2,'x'=4,'y'=4,'z'=16] {'z'}, dimensions={0} | all-to-all | bytes 147456 | tf_op jit(solution)/shard_map/all_to_all | solution.py:212
  89.0 0.8 finish.1
  (4 shorter events, 0.1 us)
Async XLA Ops:
  5.9 27.0 %all-to-all-start = ((bf16[16,16,128]{2,1,0:T(8,128)(2,1)}), bf16[16,16,128]{2,1,0:T(8,128)(2,1)S(1)}, u32[]{:S(2)}, u32[]{:S(2)}) async-start(bf16[16,16,128]{2,1,0:T(8,128)(2,1)} %get-tuple-element.8), calls=%async_computation | async-start | bytes 131072 | tf_op jit(solution)/shard_map/all_to_all | solution.py:192
  33.1 19.9 %copy-start = (bf16[256,2048]{1,0:T(8,128)(2,1)S(1)}, bf16[256,2048]{1,0:T(8,128)(2,1)}, u32[]{:S(2)}) copy-start(bf16[256,2048]{1,0:T(8,128)(2,1)} %images_ref.1) | copy-start | bytes 3145732
  33.1 19.9 %copy-start.1 = (f32[256]{0:T(256)S(1)}, f32[256]{0:T(256)}, u32[]{:S(2)}) copy-start(f32[256]{0:T(256)} %param.9) | copy-start | bytes 3076
  33.1 19.9 %copy-start.2 = (bf16[256,1024]{1,0:T(8,128)(2,1)S(1)}, bf16[256,1024]{1,0:T(8,128)(2,1)}, u32[]{:S(2)}) copy-start(bf16[256,1024]{1,0:T(8,128)(2,1)} %pick_second.1.picked_ref) | copy-start | bytes 1572868
